TPU v7x, 32 devices: a whole 2x2x4 slice. The times are simulated.
32 devices in a mesh: sub: 8 (over y, x, core), grp: 4 (over z).
Axes of the slice: x: 2, y: 2, z: 4, core: 2. Of those that a mesh axis runs over, the one named last changes fastest.
Arguments:
- forces: float32 [8, 4, 750, 128], P('sub', 'grp'), may hold values from -52 to 52
- stiffness: bfloat16 [375, 375], replicated, may hold values from -0.0108443534 to 0.61, as said below
- local_solve: bfloat16 [375, 375], replicated, may hold values from -0.01600833 to 0.91, as said below
- moduli: float32 [8, 4, 4], P('sub', 'grp'), may hold values from 0.25 to 2.5
- coarse_basis: float32 [8, 4, 750], P('sub', 'grp'), may hold values from -0.21875 to 0.21875
- coarse_inverse: float32 [32, 32], P(('sub', 'grp')), may hold values from -2.4206146 to 41.079192, as said below
- send_index: int32 [8, 4, 4, 316], P('sub', 'grp'), may hold values from 0 to 1500, as said below
- owner_slot: int32 [8, 4, 4, 316], P('sub', 'grp'), may hold values from 0 to 750, as said below
- home_slot: int32 [8, 4, 1500], P('sub', 'grp'), may hold values from 0 to 750, as said below
Outputs:
- solution: float32 [8, 4, 750, 128], P('sub', 'grp')
- residual: float32 [8, 4, 750, 128], P('sub', 'grp')
Inputs may be any that keep to these rules, and one draw needn't show every extreme that they name: For each subdomain and each member j of its slab, the used slots of the message to j (send_index below 1500) come first and unused ones hold 1500. Each subdomain sends to exactly 2 other members of its slab, every such message has used slots, and the relation is symmetric; all other messages, the one to itself included, are unused. Local degrees of freedom below 750 are never sent; exactly 562 local degrees of freedom of each subdomain are sent, each in exactly one used slot; on every subdomain one message has all 316 slots used. owner_slot[s, j, i, k] is below 750 exactly where send_index[s, i, j, k] is a used slot and equals 750 elsewhere. home_slot[s, i, l] equals 750 exactly where local degree of freedom l of subdomain (s, i) is sent; every owned degree of freedom of a subdomain is read by at least one of its local degrees of freedom that are not sent. `stiffness`: symmetric positive definite. `local_solve`: symmetric positive definite. `coarse_inverse`: symmetric positive definite.
All inputs are finite; a program needn't handle non-finite values.
Results may differ from a plain program's by a relative error of at most 0.0053.
Values may be sent and summed in bfloat16 or wider, within the bound.
No kernel may reach another device: no remote copies, remote signals or barrier semaphores. Data moves between devices by JAX's collectives and lax.ppermute only.
A program may use at most 64 MiB of HBM per device.

v0:
```python
import jax
import jax.numpy as jnp
from jax import lax
from jax.sharding import PartitionSpec as P

ITERS = 2


def spread_owned(values, slot_rows):
    padded = jnp.concatenate([values, jnp.zeros((1, values.shape[1]), values.dtype)], axis=0)
    return jnp.take(padded, slot_rows, axis=0)


def element_block(copies, matrix, factors, divide):
    columns = copies.shape[-1]
    blocks = copies.reshape(factors.shape[0], matrix.shape[0], columns)
    product = jnp.einsum("ab,ebr->ear", matrix, blocks, preferred_element_type=jnp.float32)
    if divide:
        scaled = product / factors[:, None, None]
    else:
        scaled = product * factors[:, None, None]
    return scaled.astype(jnp.bfloat16).reshape(-1, columns)


def body(
    forces,
    stiffness,
    local_solve,
    moduli,
    coarse_basis,
    coarse_inverse,
    send_index,
    owner_slot,
    home_slot,
):
    loaded = forces[0, 0]
    owned_count = loaded.shape[0]
    send_rows = send_index[0, 0]
    slot_rows = owner_slot[0, 0]
    home_rows = home_slot[0, 0]
    elastic = moduli[0, 0]
    basis_values = coarse_basis[0, 0]
    groups, capacity = send_rows.shape
    block_size = stiffness.shape[0]
    inner_count = elastic.shape[0] // 2
    border_start = inner_count * block_size
    local_count = home_rows.shape[0]
    inner_elastic = elastic[:inner_count]
    outer_elastic = elastic[inner_count:]
    sent_position = (
        jnp.zeros((local_count + 1,), jnp.int32)
        .at[send_rows.reshape(-1)]
        .set(jnp.arange(groups * capacity, dtype=jnp.int32))[:local_count]
    )
    position = jnp.where(home_rows < owned_count, groups * capacity + home_rows, sent_position)
    inner_home = home_rows[:border_start]
    outer_rows = position[border_start:]
    gather_rows = jnp.concatenate([slot_rows.reshape(-1), home_rows], axis=0)
    device = lax.axis_index(("sub", "grp"))
    full_inverse = lax.all_gather(coarse_inverse, ("sub", "grp"), axis=0, tiled=True)

    def joined(received, own_values):
        columns = received.shape[2]
        return jnp.concatenate([received.reshape(-1, columns), own_values], axis=0)

    def return_terms(inner_terms, outer_copies, matrix, divide):
        outer_terms = element_block(outer_copies, matrix, outer_elastic, divide)
        element_terms = jnp.concatenate([inner_terms, outer_terms], axis=0)
        columns = element_terms.shape[1]
        padded = jnp.concatenate(
            [element_terms, jnp.zeros((1, columns), element_terms.dtype)], axis=0
        )
        outgoing = jnp.take(padded, send_rows, axis=0)
        returned = lax.all_to_all(outgoing, "grp", split_axis=0, concat_axis=0, tiled=True)
        contributions = jnp.concatenate(
            [returned.reshape(-1, columns), element_terms], axis=0
        ).astype(jnp.float32)
        summed = (
            jnp.zeros((owned_count + 1, columns), jnp.float32).at[gather_rows].add(contributions)
        )
        return summed[:owned_count]

    def residual_solve(residual):
        own_copy = residual.astype(jnp.bfloat16)
        inner_terms = element_block(
            jnp.take(own_copy, inner_home, axis=0), local_solve, inner_elastic, True
        )
        received = lax.all_to_all(
            spread_owned(own_copy, slot_rows), "grp", split_axis=0, concat_axis=0, tiled=True
        )
        outer_copies = jnp.take(joined(received, own_copy), outer_rows, axis=0)
        return return_terms(inner_terms, outer_copies, local_solve, True)

    def coarse_step(residual, local_part):
        own_term = jnp.dot(basis_values[None, :], residual, precision=lax.Precision.HIGHEST)
        spread = jnp.zeros((full_inverse.shape[0], own_term.shape[1]), jnp.float32)
        spread = lax.dynamic_update_slice(spread, own_term, (device, jnp.int32(0)))
        totals, partial_value = lax.psum(
            (spread, jnp.sum(residual * local_part, axis=0)), ("sub", "grp")
        )
        answer = jnp.dot(full_inverse, totals, precision=lax.Precision.HIGHEST)
        own_answer = lax.dynamic_slice_in_dim(answer, device, 1, 0)
        search = local_part + basis_values[:, None] * own_answer
        weighted = partial_value + jnp.sum(totals * answer, axis=0)
        return (search, weighted)

    solution = jnp.zeros_like(loaded)
    residual = loaded
    local_part = residual_solve(residual)
    search, weighted = coarse_step(residual, local_part)
    direction = search
    for iteration in range(ITERS):
        apply_own_copy = direction.astype(jnp.bfloat16)
        apply_inner_terms = element_block(
            jnp.take(apply_own_copy, inner_home, axis=0), stiffness, inner_elastic, False
        )
        apply_received = lax.all_to_all(
            spread_owned(apply_own_copy, slot_rows), "grp", split_axis=0, concat_axis=0, tiled=True
        )
        apply_outer_copies = jnp.take(joined(apply_received, apply_own_copy), outer_rows, axis=0)
        image_field = return_terms(apply_inner_terms, apply_outer_copies, stiffness, False)
        final_turn = iteration + 1 == ITERS
        curvature = lax.psum(jnp.sum(direction * image_field, axis=0), ("sub", "grp"))
        step_size = weighted / curvature
        solution = solution + step_size[None, :] * direction
        residual = residual - step_size[None, :] * image_field
        if not final_turn:
            local_part = residual_solve(residual)
            search, update = coarse_step(residual, local_part)
            direction = search + (update / weighted)[None, :] * direction
            weighted = update
    return (solution[None, None], residual[None, None])


def solution(mesh):
    return jax.shard_map(
        body,
        mesh=mesh,
        in_specs=(
            P("sub", "grp", None, None),
            P(),
            P(),
            P("sub", "grp", None),
            P("sub", "grp", None),
            P(("sub", "grp"), None),
            P("sub", "grp", None, None),
            P("sub", "grp", None, None),
            P("sub", "grp", None),
        ),
        out_specs=(P("sub", "grp", None, None), P("sub", "grp", None, None)),
        check_vma=False,
    )
```

profile of v0, /device:TPU:0, one launch (start us, length us, event | category | flops | bytes accessed | tf_op | source)
XLA Modules:
  0.0 452.3 jit_solution(18298687678526419312)
XLA Ops:
  3.2 3.0 gather_fusion.1
  7.3 6.3 %all-to-all-start = ((bf16[4,316,128]{2,1,0:T(8,128)(2,1)}), bf16[4,316,128]{2,1,0:T(8,128)(2,1)S(1)}, u32[]{:S(2)}, u32[]{:S(2)}) async-start(bf16[4,316,128]{2,1,0:T(8,128)(2,1)} %broadcast_select_fusion.7), calls=%async_computation | async-start | bytes 655360 | tf_op jit(solution)/shard_map/all_to_all | solution.py:88
  16.2 6.4 %scatter_custom_fusion = s32[1501]{0:T(1024)S(1)} fusion(s32[1264]{0:T(1024)S(1)} %fusion.43, s32[1264]{0:T(1024)S(1)} %iota.3, s32[]{:T(128)} %constant.45.clone.1), kind=kCustom, calls=%fused_computation.120 | custom fusion | bytes 6008 | tf_op jit(solution)/shard_map/scatter | solution.py:53
  31.9 4.9 %all-to-all-start.1 = ((bf16[4,316,128]{2,1,0:T(8,128)(2,1)}), bf16[4,316,128]{2,1,0:T(8,128)(2,1)S(1)}, u32[]{:S(2)}, u32[]{:S(2)}) async-start(bf16[4,316,128]{2,1,0:T(8,128)(2,1)} %broadcast_select_fusion.3), calls=%async_computation.1 | async-start | bytes 655360 | tf_op jit(solution)/shard_map/all_to_all | solution.py:74
  37.1 67.0 %all-gather = f32[32,1,32]{2,1,0:T(1,128)S(1)} all-gather(f32[1,1,32]{2,1,0:T(1,128)S(1)} %bitcast.103), channel_id=1, replica_groups=mesh['sub'=8,'grp'=4] {'sub','grp'}, dimensions={0}, use_global_device_ids=true | all-gather | bytes 4224 | tf_op jit(solution)/shard_map/all_gather | solution.py:60
  104.2 37.3 %psum.43 = f32[32,128]{1,0:T(8,128)S(1)} all-reduce(f32[32,128]{1,0:T(8,128)S(1)} %dynamic_update_slice.6), channel_id=1, replica_groups=mesh['sub'=8,'grp'=4] {'sub','grp'}, use_global_device_ids=true, to_apply=%region_4.9 | all-reduce | flops 4096 | bytes 32768 | tf_op jit(solution)/shard_map/psum | solution.py:98
  143.4 18.1 %scatter_custom_fusion.1 = f32[751,128]{1,0:T(8,128)S(1)} fusion(s32[2764]{0:T(1024)S(1)} %fusion.42, bf16[2764,128]{1,0:T(8,128)(2,1)S(1)} %concatenate.92, f32[]{:T(128)} %constant.44.clone.1), kind=kCustom, calls=%fused_computation.27 | custom fusion | flops 707584 | bytes 1093124 | tf_op jit(solution)/shard_map/scatter-add | solution.py:79
  165.7 3.9 all-to-all-start.2
  173.0 6.0 %all-to-all-done.2 = bf16[4,316,128]{2,1,0:T(8,128)(2,1)S(1)} async-done(((bf16[4,316,128]{2,1,0:T(8,128)(2,1)}), bf16[4,316,128]{2,1,0:T(8,128)(2,1)S(1)}, u32[]{:S(2)}, u32[]{:S(2)}) %all-to-all-start.2) | async-done | bytes 323616 | tf_op jit(solution)/shard_map/all_to_all | solution.py:117
  186.2 13.2 %all_to_all.40 = bf16[4,316,128]{2,1,0:T(8,128)(2,1)S(1)} all-to-all(bf16[4,316,128]{2,1,0:T(8,128)(2,1)S(1)} %broadcast_select_fusion.2), channel_id=1, replica_groups=mesh['sub'=8,'grp'=4] {'grp'}, dimensions={0} | all-to-all | bytes 647168 | tf_op jit(solution)/shard_map/all_to_all | solution.py:74
  201.0 18.1 %scatter_custom_fusion.2 = f32[751,128]{1,0:T(8,128)S(1)} fusion(s32[2764]{0:T(1024)S(1)} %fusion.42, bf16[2764,128]{1,0:T(8,128)(2,1)S(1)} %concatenate.96, f32[]{:T(128)} %constant.44.clone.1), kind=kCustom, calls=%fused_computation.25 | custom fusion | flops 707584 | bytes 1093124 | tf_op jit(solution)/shard_map/scatter-add | solution.py:79
  219.3 39.0 %all-reduce.5 = (f32[128]{0:T(128)S(1)}, f32[128]{0:T(128)S(1)}) all-reduce(f32[128]{0:T(128)S(1)} %get-tuple-element.13, f32[128]{0:T(128)S(1)} %get-tuple-element.12), channel_id=1, replica_groups=mesh['sub'=8,'grp'=4] {'sub','grp'}, use_global_device_ids=true, to_apply=%region_3.8 | all-reduce | flops 256 | bytes 2048 | tf_op jit(solution)/shard_map/psum | solution.py:98
  258.4 3.0 gather_fusion.9
  262.4 3.5 all-to-all-start.4
  268.5 7.1 %all-to-all-done.4 = bf16[4,316,128]{2,1,0:T(8,128)(2,1)S(1)} async-done(((bf16[4,316,128]{2,1,0:T(8,128)(2,1)}), bf16[4,316,128]{2,1,0:T(8,128)(2,1)S(1)}, u32[]{:S(2)}, u32[]{:S(2)}) %all-to-all-start.4) | async-done | bytes 323616 | tf_op jit(solution)/shard_map/all_to_all | solution.py:88
  283.5 3.5 all-to-all-start.5
  287.6 8.0 %all-to-all-done.5 = bf16[4,316,128]{2,1,0:T(8,128)(2,1)S(1)} async-done(((bf16[4,316,128]{2,1,0:T(8,128)(2,1)}), bf16[4,316,128]{2,1,0:T(8,128)(2,1)S(1)}, u32[]{:S(2)}, u32[]{:S(2)}) %all-to-all-start.5) | async-done | bytes 323616 | tf_op jit(solution)/shard_map/all_to_all | solution.py:74
  297.3 18.1 %scatter_custom_fusion.3 = f32[751,128]{1,0:T(8,128)S(1)} fusion(s32[2764]{0:T(1024)S(1)} %fusion.42, bf16[2764,128]{1,0:T(8,128)(2,1)S(1)} %concatenate.100, f32[]{:T(128)} %constant.44.clone.1), kind=kCustom, calls=%fused_computation.23 | custom fusion | flops 707584 | bytes 1093124 | tf_op jit(solution)/shard_map/scatter-add | solution.py:79
  315.5 38.9 %all-reduce.4 = (f32[128]{0:T(128)S(1)}, f32[32,128]{1,0:T(8,128)S(1)}) all-reduce(f32[128]{0:T(128)S(1)} %multiply_reduce_fusion.1, f32[32,128]{1,0:T(8,128)S(1)} %dynamic_update_slice.7), channel_id=1, replica_groups=mesh['sub'=8,'grp'=4] {'sub','grp'}, use_global_device_ids=true, to_apply=%region_11.16 | all-reduce | flops 4224 | bytes 33792 | tf_op jit(solution)/shard_map/psum | solution.py:98
  358.8 3.5 all-to-all-start.6
  364.9 7.1 %all-to-all-done.6 = bf16[4,316,128]{2,1,0:T(8,128)(2,1)S(1)} async-done(((bf16[4,316,128]{2,1,0:T(8,128)(2,1)}), bf16[4,316,128]{2,1,0:T(8,128)(2,1)S(1)}, u32[]{:S(2)}, u32[]{:S(2)}) %all-to-all-start.6) | async-done | bytes 323616 | tf_op jit(solution)/shard_map/all_to_all | solution.py:117
  379.2 11.9 %all_to_all.41 = bf16[4,316,128]{2,1,0:T(8,128)(2,1)S(1)} all-to-all(bf16[4,316,128]{2,1,0:T(8,128)(2,1)S(1)} %broadcast_select_fusion), channel_id=1, replica_groups=mesh['sub'=8,'grp'=4] {'grp'}, dimensions={0} | all-to-all | bytes 647168 | tf_op jit(solution)/shard_map/all_to_all | solution.py:74
  392.8 18.1 %scatter_custom_fusion.4 = f32[751,128]{1,0:T(8,128)S(1)} fusion(s32[2764]{0:T(1024)S(1)} %fusion.42, bf16[2764,128]{1,0:T(8,128)(2,1)S(1)} %concatenate.104, f32[]{:T(128)} %constant.44.clone.1), kind=kCustom, calls=%fused_computation.21 | custom fusion | flops 707584 | bytes 1093124 | tf_op jit(solution)/shard_map/scatter-add | solution.py:79
  411.0 38.8 %psum.47 = f32[128]{0:T(128)S(1)} all-reduce(f32[128]{0:T(128)S(1)} %multiply_reduce_fusion), channel_id=1, replica_groups=mesh['sub'=8,'grp'=4] {'sub','grp'}, use_global_device_ids=true, to_apply=%region_16.21 | all-reduce | flops 128 | bytes 1024 | tf_op jit(solution)/shard_map/psum | solution.py:123
  (153 shorter events, 66.1 us)
Async XLA Ops:
  0.6 22.1 %copy-start = (bf16[375,375]{1,0:T(8,128)(2,1)S(1)}, bf16[375,375]{1,0:T(8,128)(2,1)}, u32[]{:S(2)}) copy-start(bf16[375,375]{1,0:T(8,128)(2,1)} %param.19) | copy-start | bytes 843754
  6.3 7.3 %copy-start.3 = (s32[1,1,1500]{2,1,0:T(1,128)S(1)}, s32[1,1,1500]{2,1,0:T(1,128)}, u32[]{:S(2)}) copy-start(s32[1,1,1500]{2,1,0:T(1,128)} %param.25) | copy-start | bytes 18004
  6.3 7.4 %copy-start.5 = (s32[1,1,4,316]{3,2,1,0:T(4,128)S(1)}, s32[1,1,4,316]{3,2,1,0:T(4,128)}, u32[]{:S(2)}) copy-start(s32[1,1,4,316]{3,2,1,0:T(4,128)} %param.23) | copy-start | bytes 15172
  6.3 7.5 %copy-start.7 = (f32[1,1,4]{2,1,0:T(1,128)S(1)}, f32[1,1,4]{2,1,0:T(1,128)}, u32[]{:S(2)}) copy-start(f32[1,1,4]{2,1,0:T(1,128)} %param.20) | copy-start | bytes 52
  7.3 16.6 %all-to-all-start = ((bf16[4,316,128]{2,1,0:T(8,128)(2,1)}), bf16[4,316,128]{2,1,0:T(8,128)(2,1)S(1)}, u32[]{:S(2)}, u32[]{:S(2)}) async-start(bf16[4,316,128]{2,1,0:T(8,128)(2,1)} %broadcast_select_fusion.7), calls=%async_computation | async-start | bytes 655360 | tf_op jit(solution)/shard_map/all_to_all | solution.py:88
  22.8 0.7 copy-start.4
  22.8 0.9 copy-start.6
  30.9 5.9 %copy-start.1 = (f32[1,1,750,128]{3,1,2,0:T(1,128)S(1)}, f32[1,1,750,128]{3,1,2,0:T(1,128)}, u32[]{:S(2)}) copy-start(f32[1,1,750,128]{3,1,2,0:T(1,128)} %param.17) | copy-start | bytes 1152004
  30.9 6.3 %copy-start.8 = (f32[1,32]{1,0:T(1,128)S(1)}, f32[1,32]{1,0:T(1,128)}, u32[]{:S(2)}) copy-start(f32[1,32]{1,0:T(1,128)} %param.22) | copy-start | bytes 388
  31.9 109.8 %all-to-all-start.1 = ((bf16[4,316,128]{2,1,0:T(8,128)(2,1)}), bf16[4,316,128]{2,1,0:T(8,128)(2,1)S(1)}, u32[]{:S(2)}, u32[]{:S(2)}) async-start(bf16[4,316,128]{2,1,0:T(8,128)(2,1)} %broadcast_select_fusion.3), calls=%async_computation.1 | async-start | bytes 655360 | tf_op jit(solution)/shard_map/all_to_all | solution.py:74
  165.7 13.3 %all-to-all-start.2 = ((bf16[4,316,128]{2,1,0:T(8,128)(2,1)}), bf16[4,316,128]{2,1,0:T(8,128)(2,1)S(1)}, u32[]{:S(2)}, u32[]{:S(2)}) async-start(bf16[4,316,128]{2,1,0:T(8,128)(2,1)} %broadcast_select_fusion.6), calls=%async_computation.2 | async-start | bytes 655360 | tf_op jit(solution)/shard_map/all_to_all | solution.py:117
  171.7 1.0 copy-start.2
  262.4 13.2 %all-to-all-start.4 = ((bf16[4,316,128]{2,1,0:T(8,128)(2,1)}), bf16[4,316,128]{2,1,0:T(8,128)(2,1)S(1)}, u32[]{:S(2)}, u32[]{:S(2)}) async-start(bf16[4,316,128]{2,1,0:T(8,128)(2,1)} %broadcast_select_fusion.5), calls=%async_computation.4 | async-start | bytes 655360 | tf_op jit(solution)/shard_map/all_to_all | solution.py:88
  283.5 12.1 %all-to-all-start.5 = ((bf16[4,316,128]{2,1,0:T(8,128)(2,1)}), bf16[4,316,128]{2,1,0:T(8,128)(2,1)S(1)}, u32[]{:S(2)}, u32[]{:S(2)}) async-start(bf16[4,316,128]{2,1,0:T(8,128)(2,1)} %broadcast_select_fusion.1), calls=%async_computation.5 | async-start | bytes 655360 | tf_op jit(solution)/shard_map/all_to_all | solution.py:74
  358.8 13.2 %all-to-all-start.6 = ((bf16[4,316,128]{2,1,0:T(8,128)(2,1)}), bf16[4,316,128]{2,1,0:T(8,128)(2,1)S(1)}, u32[]{:S(2)}, u32[]{:S(2)}) async-start(bf16[4,316,128]{2,1,0:T(8,128)(2,1)} %broadcast_select_fusion.4), calls=%async_computation.6 | async-start | bytes 655360 | tf_op jit(solution)/shard_map/all_to_all | solution.py:117
where the time goes:
time: 453 us; the launch traced here: 452 us
  blocking collectives  246 us (54%)
  other arithmetic  83 us (18%)
  local copies, waits for them, and re-layouts  64.7 us (14%)
  waiting for transfers between devices  28.5 us (6%)
  starting transfers between devices  25.5 us (6%)
    psum x3, blocking collectives, coarse_step(): lax.psum((spread, jnp.sum(residual * local_part, axis=0)), ('sub', 'grp'))  115 us
    scatter-add x4, other arithmetic, return_terms(): jnp.zeros((owned_count + 1, columns), jnp.float32).at[gather_rows]  72.5 us
    all_gather x1, blocking collectives, body(): lax.all_gather(coarse_inverse, ('sub', 'grp'), axis=0, tiled=True)  67 us
    psum x1, blocking collectives, body(): lax.psum(jnp.sum(direction * image_field, axis=0), ('sub', 'grp'))  38.8 us
    all_to_all x2, blocking collectives, return_terms(): lax.all_to_all(outgoing, 'grp', split_axis=0, concat_axis=0, tiled=True)  25 us
    all_to_all x2, waiting for transfers between devices, body(): lax.all_to_all(spread_owned(apply_own_copy, slot_rows), 'grp', split_axis...  13.2 us
    gather x8, local copies, waits for them, and re-layouts, spread_owned(): return jnp.take(padded, slot_rows, axis=0)  12.3 us
    gather x8, local copies, waits for them, and re-layouts, return_terms(): outgoing = jnp.take(padded, send_rows, axis=0)  12.2 us
  transfers between devices with their start and end apart: 6, of which 5 were waited for; matrix products, arithmetic and copies ran while one was open for 4% of the time, Pallas kernels for 0%

commit v1 on v0

--- a/solution.py
+++ b/solution.py
@@ -1,9 +1,443 @@
+import functools
+
 import jax
 import jax.numpy as jnp
 from jax import lax
+from jax.experimental import pallas as pl
+from jax.experimental.pallas import tpu as pltpu
 from jax.sharding import PartitionSpec as P
 
 ITERS = 2
+LANES = 128
+RIDERS = 16
+
+
+def round_up(value, unit):
+    return -(-value // unit) * unit
+
+
+PLACES = 4
+
+
+def place_distance(order_ref, place):
+    return 0 if place == 0 else order_ref[place - 1]
+
+
+def slab_kernel(
+    order_ref,
+    x0_ref,
+    x1_ref,
+    x2_ref,
+    x3_ref,
+    t0_ref,
+    t1_ref,
+    t2_ref,
+    t3_ref,
+    coarse_ref,
+    inverse_ref,
+    matrices_ref,
+    basis_ref,
+    fields_ref,
+    images_ref,
+    gram_ref,
+    tables,
+    slots,
+    sources,
+    sources_t,
+    pick,
+    put,
+    values,
+    terms,
+    own,
+    riders,
+    factors,
+    square,
+):
+    owned = values.shape[3]
+    half = pick.shape[2]
+    block = matrices_ref.shape[1]
+    loads = fields_ref.shape[1]
+    slot_count = slots.shape[1]
+    f32, bf16 = jnp.float32, jnp.bfloat16
+    distance = [place_distance(order_ref, place) for place in range(PLACES)]
+
+    for at, (x_ref, t_ref) in enumerate(
+        ((x0_ref, t0_ref), (x1_ref, t1_ref), (x2_ref, t2_ref), (x3_ref, t3_ref))
+    ):
+        terms[0, at] = x_ref[...]
+        tables[at] = t_ref[...]
+    row_ids = lax.broadcasted_iota(jnp.int32, (RIDERS, owned), 0)
+    sources[...] = jnp.full(sources.shape, -1.0, f32)
+    slots[...] = jnp.full(slots.shape, -1.0, f32)
+    for place in range(PLACES):
+        table = tables[distance[place]]
+        values[0, place] = terms[0, distance[place]]
+        riders[place] = jnp.where(
+            row_ids == place, values[0, place, loads : loads + 1, :].astype(f32), 0.0
+        ).astype(bf16)
+        factors[0, place] = table[6:8, :]
+        factors[1, place] = 1.0 / table[6:8, :]
+        sources[place : place + 1, :] = table[0:1, :]
+        sources[PLACES + place : PLACES + place + 1, :] = table[1:2, :]
+
+    pairs = [(a, (a + step) % PLACES) for step in (1, PLACES - 1) for a in range(PLACES)]
+    for pair, (reader, owner) in enumerate(pairs):
+        row = pl.ds(2 + (distance[reader] ^ distance[owner]), 1)
+        slots[2 * pair : 2 * pair + 1, :] = tables[distance[reader], row, :slot_count]
+        slots[2 * pair + 1 : 2 * pair + 2, :] = tables[distance[owner], row, slot_count:]
+    slots_t = slots[...].T
+    half_ids = lax.broadcasted_iota(jnp.int32, (LANES, half), 1).astype(f32)
+    for pair in range(len(pairs)):
+        found = jnp.zeros((1, half), f32)
+        for start in range(0, slot_count, LANES):
+            sent = slots_t[start : start + LANES, 2 * pair : 2 * pair + 1]
+            target = slots_t[start : start + LANES, 2 * pair + 1 : 2 * pair + 2] + 1.0
+            found = found + jnp.sum(
+                jnp.where(half_ids == sent, target, 0.0), axis=0, keepdims=True
+            )
+        sources[2 * PLACES + pair : 2 * PLACES + pair + 1, :] = found - 1.0
+    sources_t[...] = sources[...].T
+
+    chunk = 256
+    lane_ids = lax.broadcasted_iota(jnp.int32, (chunk, owned), 1).astype(f32)
+    deep_ids = lax.broadcasted_iota(jnp.int32, (chunk, half), 0).astype(f32)
+    column_ids = lax.broadcasted_iota(jnp.int32, (chunk, LANES), 1)
+
+    def build(n, carry):
+        source = sources[pl.ds(n, 1), :]
+        for start in range(0, owned, chunk):
+            pick[n, start : start + chunk, :] = jnp.where(
+                deep_ids == source - float(start), 1.0, 0.0
+            ).astype(bf16)
+        for start in range(0, half, chunk):
+            column = jnp.sum(
+                jnp.where(column_ids == n, sources_t[start : start + chunk, :], 0.0),
+                axis=1,
+                keepdims=True,
+            )
+            put[n, start : start + chunk, :] = jnp.where(lane_ids == column, 1.0, 0.0).astype(bf16)
+        return carry
+
+    lax.fori_loop(0, 4 * PLACES, build, 0)
+
+    def multiply(left, right):
+        return jnp.dot(left, right, preferred_element_type=f32)
+
+    def element(which, place, part, copies):
+        rounded = copies.astype(bf16)
+        for start in range(0, half, block):
+            product = multiply(rounded[:, start : start + block], matrices_ref[which])
+            scale = factors[which, place, part : part + 1, start : start + block]
+            terms[part, place, :, start : start + block] = (product * scale).astype(bf16)
+
+    def around(place, step):
+        return lax.rem(place + step, PLACES)
+
+    def inner(which, source, place):
+        element(which, place, 0, multiply(values[source, place], pick[place]))
+
+    def outer(which, source, place):
+        ahead, behind = around(place, 1), around(place, PLACES - 1)
+        copies = (
+            multiply(values[source, place], pick[PLACES + place])
+            + multiply(values[source, ahead], pick[2 * PLACES + place])
+            + multiply(values[source, behind], pick[3 * PLACES + place])
+        )
+        element(which, place, 1, copies)
+
+    def collect(place):
+        ahead, behind = around(place, 1), around(place, PLACES - 1)
+        return (
+            multiply(terms[0, place], put[place])
+            + multiply(terms[1, place], put[PLACES + place])
+            + multiply(terms[1, behind], put[2 * PLACES + behind])
+            + multiply(terms[1, ahead], put[3 * PLACES + ahead])
+        )
+
+    def stage(at, carry):
+        which = lax.rem(at + 1, 2)
+        source, target = lax.rem(at, 2), lax.rem(at + 1, 2)
+
+        def spread(place, inside):
+            inner(which, source, place)
+            outer(which, source, place)
+            return inside
+
+        def gather(place, inside):
+            summed = collect(place)
+            values[target, place] = summed.astype(bf16)
+
+            @pl.when(place == 0)
+            def _():
+                own[at] = summed
+
+            return inside
+
+        lax.fori_loop(0, PLACES, spread, 0)
+        lax.fori_loop(0, PLACES, gather, 0)
+
+        @pl.when(at == 0)
+        def _():
+            for place in range(PLACES):
+                values[1, place, loads:, :] = riders[place]
+
+        return carry
+
+    lax.fori_loop(0, 3, stage, 0)
+    inner(0, 1, 0)
+    outer(0, 1, 0)
+    outer(0, 1, 1)
+    outer(0, 1, 3)
+    own[3] = collect(0)
+
+    first = order_ref[4] * PLACES
+    member = order_ref[3]
+    square[...] = jnp.zeros_like(square)
+    for place in range(PLACES):
+        square[place : place + 1, : inverse_ref.shape[1]] = inverse_ref[
+            pl.ds(first + (member ^ distance[place]), 1), :
+        ]
+    answer = jnp.dot(
+        square[0:8, : inverse_ref.shape[1]],
+        coarse_ref[...],
+        precision=lax.Precision.HIGHEST,
+        preferred_element_type=f32,
+    )
+    square[...] = jnp.zeros_like(square)
+    square[0:8, :] = answer
+    answer_t = square[...].T
+    basis = basis_ref[...]
+    start_field = own[0, :loads, :] + answer_t[:, 0:1] * basis
+    start_image = own[1, :loads, :]
+    next_field = own[2, :loads, :]
+    next_image = own[3, :loads, :]
+    for place in range(PLACES):
+        column = answer_t[:, place : place + 1]
+        row = loads + place
+        start_image = start_image + column * own[1, row : row + 1, :]
+        next_field = next_field + column * own[2, row : row + 1, :]
+        next_image = next_image + column * own[3, row : row + 1, :]
+    fields_ref[0] = start_field
+    fields_ref[1] = next_field
+    fields_ref[2] = start_image
+    fields_ref[3] = next_image
+    images_ref[...] = own[1, loads : loads + 8, :]
+    residual = x0_ref[:loads, :].astype(f32)
+    lanes = lax.broadcasted_iota(jnp.int32, square.shape, 1)
+    collected = jnp.zeros(square.shape, f32)
+    for at, product in enumerate(
+        (
+            residual * start_field,
+            start_field * start_image,
+            start_image * next_field,
+            next_field * next_image,
+            basis * start_image,
+            basis * next_image,
+        )
+    ):
+        total = jnp.sum(product, axis=1, keepdims=True)
+        collected = jnp.where(lanes == at, total, collected)
+    gram = collected.T[0:8, :]
+    row_at = lax.broadcasted_iota(jnp.int32, gram.shape, 0)
+    lane_at = lax.broadcasted_iota(jnp.int32, gram.shape, 1)
+    for place in range(PLACES):
+        entry = jnp.sum(
+            basis * own[1, loads + place : loads + place + 1, :], axis=1, keepdims=True
+        )
+        here = (row_at == 6) & (lane_at == first + (member ^ distance[place]))
+        gram = jnp.where(here, entry, gram)
+    gram_ref[...] = gram
+
+
+def finish_kernel(
+    order_ref,
+    gram_ref,
+    inverse_ref,
+    fields_ref,
+    images_ref,
+    basis_ref,
+    forces_ref,
+    solution_ref,
+    residual_ref,
+    answer,
+    square,
+):
+    f32 = jnp.float32
+    count = inverse_ref.shape[0]
+    owned = forces_ref.shape[0]
+    first = order_ref[4] * PLACES
+    member = order_ref[3]
+    precise = functools.partial(
+        jnp.dot, precision=lax.Precision.HIGHEST, preferred_element_type=f32
+    )
+    coarse = gram_ref[:, 4, :]
+    answer[...] = precise(inverse_ref[...], coarse)
+    answers = answer[...]
+    mixed = precise(gram_ref[:, 6, :count], answers)
+    sums = jnp.sum(gram_ref[...], axis=0)
+    weighted, curvature = sums[0:1, :], sums[1:2, :]
+    cross = sums[2:3, :] + jnp.sum(coarse * answers, axis=0, keepdims=True)
+    last = sums[3:4, :] + jnp.sum(
+        answers * (2.0 * gram_ref[:, 5, :] + mixed), axis=0, keepdims=True
+    )
+    step = weighted / curvature
+    update = step * step * cross - weighted
+    grown = 1.0 + update / weighted
+    curvature = grown * grown * curvature - 2.0 * step * grown * cross + step * step * last
+    second = update / curvature
+    whole = step + second * grown
+    back = step * second
+    square[...] = jnp.zeros_like(square)
+    square[0:1, :] = whole
+    square[1:2, :] = back
+    for place in range(PLACES):
+        at = first + (member ^ place_distance(order_ref, place))
+        square[2 + place : 3 + place, :] = back * answer[pl.ds(at, 1), :]
+    columns = square[...].T
+    whole, back = columns[:, 0:1], columns[:, 1:2]
+    for start in range(0, basis_ref.shape[1], LANES):
+        part = slice(start, start + LANES)
+        size = min(LANES, owned - start)
+        iterate = (
+            whole * fields_ref[0, :, part]
+            - back * fields_ref[1, :, part]
+            - columns[:, 2:3] * basis_ref[:, part]
+        )
+        change = back * fields_ref[3, :, part] - whole * fields_ref[2, :, part]
+        for place in range(PLACES):
+            change = (
+                change + columns[:, 2 + place : 3 + place] * images_ref[place : place + 1, part]
+            )
+        rows = slice(start, start + size)
+        solution_ref[rows, :] = iterate.T[:size]
+        residual_ref[rows, :] = forces_ref[rows, :] + change.T[:size]
+
+
+def slab_body(
+    mesh_shape,
+    forces,
+    stiffness,
+    local_solve,
+    moduli,
+    coarse_basis,
+    coarse_inverse,
+    send_index,
+    owner_slot,
+    home_slot,
+):
+    f32, bf16 = jnp.float32, jnp.bfloat16
+    axes = ("sub", "grp")
+    loaded = forces[0, 0]
+    owned_count, loads = loaded.shape
+    elements = moduli.shape[2]
+    size = stiffness.shape[0]
+    local_count = home_slot.shape[2]
+    inner_count = elements // 2
+    owned_wide = round_up(owned_count, 256)
+    block = round_up(size, LANES)
+    half = (elements - inner_count) * block
+    slot_wide = half // 2
+    devices = mesh_shape["sub"] * mesh_shape["grp"]
+    slab = lax.axis_index("sub")
+    member = lax.axis_index("grp")
+    distances = jnp.arange(PLACES, dtype=jnp.int32)
+
+    basis = jnp.pad(coarse_basis[0, 0], (0, owned_wide - owned_count))[None, :]
+    turned = jnp.pad(loaded.astype(bf16), ((0, owned_wide - owned_count), (0, 0))).T
+    packed = jnp.concatenate(
+        [turned, basis.astype(bf16), jnp.zeros((RIDERS - 1, owned_wide), bf16)], axis=0
+    )
+
+    own_term = jnp.dot(
+        coarse_basis[0, 0][None, :], loaded, precision=lax.Precision.HIGHEST
+    )
+    inverse_row = jnp.pad(coarse_inverse, ((0, 0), (0, LANES - coarse_inverse.shape[1])))
+    shared = jnp.broadcast_to(
+        jnp.concatenate([own_term, inverse_row], axis=0)[None], (devices, 2, LANES)
+    )
+
+    home = home_slot[0, 0].reshape(elements, size)
+    home = jnp.where(home < owned_count, home, -1).astype(f32)
+    home = jnp.pad(home, ((0, 0), (0, block - size)), constant_values=-1.0).reshape(2, half)
+    sent = jnp.take(send_index[0, 0], member ^ distances, axis=0)
+    used = sent[:, 0] < local_count
+    column = (sent // size - inner_count) * block + sent % size
+    column = jnp.where(sent < local_count, column, -1).astype(f32)
+    target = jnp.take(owner_slot[0, 0], member ^ distances, axis=0)
+    target = jnp.where(target < owned_count, target, -1).astype(f32)
+    spare = ((0, 0), (0, slot_wide - column.shape[1]))
+    routes = jnp.concatenate(
+        [
+            jnp.pad(column, spare, constant_values=-1.0),
+            jnp.pad(target, spare, constant_values=-1.0),
+        ],
+        axis=1,
+    )
+    modulus = jnp.broadcast_to(moduli[0, 0][:, None], (elements, block)).reshape(2, half)
+    table = jnp.concatenate([home, routes, modulus], axis=0)
+
+    opposite = jnp.sum(jnp.where(used | (distances == 0), 0, distances))
+    opposite = jnp.clip(opposite, 1, PLACES - 1)
+    near = jnp.where(opposite == 1, 2, 1)
+    order = jnp.stack(
+        [near, opposite, 6 - near - opposite, member, slab, slab, slab, slab]
+    ).astype(jnp.int32)
+
+    def swapped(array, distance):
+        return lax.ppermute(array, "grp", [(i, i ^ distance) for i in range(PLACES)])
+
+    tables = [table] + [swapped(table, d) for d in range(1, PLACES)]
+    fields = [packed] + [swapped(packed, d) for d in range(1, PLACES)]
+    shared = lax.all_to_all(shared, axes, split_axis=0, concat_axis=0, tiled=True)
+    coarse = shared[:, 0, :]
+    inverse = shared[:, 1, :devices]
+
+    widen = ((0, block - size), (0, block - size))
+    matrices = jnp.stack([jnp.pad(stiffness, widen), jnp.pad(local_solve, widen)])
+
+    rows = loads + RIDERS
+    smem = pl.BlockSpec(memory_space=pltpu.SMEM)
+    vmem = pl.BlockSpec(memory_space=pltpu.VMEM)
+    results, images, gram = pl.pallas_call(
+        slab_kernel,
+        out_shape=(
+            jax.ShapeDtypeStruct((4, loads, owned_wide), f32),
+            jax.ShapeDtypeStruct((8, owned_wide), f32),
+            jax.ShapeDtypeStruct((8, LANES), f32),
+        ),
+        in_specs=[smem] + [vmem] * 12,
+        out_specs=(vmem, vmem, vmem),
+        scratch_shapes=[
+            pltpu.VMEM((PLACES, 8, half), f32),
+            pltpu.VMEM((LANES, slot_wide), f32),
+            pltpu.VMEM((LANES, half), f32),
+            pltpu.VMEM((half, LANES), f32),
+            pltpu.VMEM((4 * PLACES, owned_wide, half), bf16),
+            pltpu.VMEM((4 * PLACES, half, owned_wide), bf16),
+            pltpu.VMEM((2, PLACES, rows, owned_wide), bf16),
+            pltpu.VMEM((2, PLACES, rows, half), bf16),
+            pltpu.VMEM((4, rows, owned_wide), f32),
+            pltpu.VMEM((PLACES, RIDERS, owned_wide), bf16),
+            pltpu.VMEM((2, PLACES, 2, half), f32),
+            pltpu.VMEM((LANES, LANES), f32),
+        ],
+        compiler_params=pltpu.CompilerParams(vmem_limit_bytes=58 * 2**20),
+        name="slab",
+    )(order, *fields, *tables, coarse, inverse, matrices, basis)
+
+    gathered = lax.all_to_all(
+        jnp.broadcast_to(gram[None], (devices, 8, LANES)), axes, 0, 0, tiled=True
+    )
+    iterate, residual = pl.pallas_call(
+        finish_kernel,
+        out_shape=(jax.ShapeDtypeStruct((owned_count, loads), f32),) * 2,
+        in_specs=[smem] + [vmem] * 6,
+        out_specs=(vmem, vmem),
+        scratch_shapes=[pltpu.VMEM((devices, LANES), f32), pltpu.VMEM((LANES, LANES), f32)],
+        compiler_params=pltpu.CompilerParams(vmem_limit_bytes=32 * 2**20),
+        name="finish",
+    )(order, gathered, inverse, results, images, basis, loaded)
+    return (iterate[None, None], residual[None, None])
 
 
 def spread_owned(values, slot_rows):
@@ -22,7 +456,7 @@
     return scaled.astype(jnp.bfloat16).reshape(-1, columns)
 
 
-def body(
+def exchange_body(
     forces,
     stiffness,
     local_solve,
@@ -133,6 +567,10 @@
 
 
 def solution(mesh):
+    if mesh.shape["grp"] == PLACES:
+        body = functools.partial(slab_body, dict(mesh.shape))
+    else:
+        body = exchange_body
     return jax.shard_map(
         body,
         mesh=mesh,

time: 453 us -> 123 us (0.27)
  blocking collectives: 246 us -> 0 us
  other arithmetic: 83 us -> 4.63 us
  Pallas kernels: 0 us -> 47.4 us
  local copies, waits for them, and re-layouts: 64.7 us -> 17.4 us
  starting transfers between devices: 25.5 us -> 16.2 us
  waiting for transfers between devices: 28.5 us -> 35 us
    psum x4 -> x0, blocking collectives: 154 us -> none  [the longest x3 115 us: coarse_step(): lax.psum((spread, jnp.sum(residual * local_part, axis=0)), ('sub', 'grp'))]
    scatter-add x4 -> x0, other arithmetic: 72.5 us -> none  [return_terms(): jnp.zeros((owned_count + 1, columns), jnp.float32).at[gather_rows]]
    all_gather x1 -> x0, blocking collectives: 67 us -> none  [body(): lax.all_gather(coarse_inverse, ('sub', 'grp'), axis=0, tiled=True)]
    pallas_call x0 -> x2, Pallas kernels: none -> 47.4 us  [the longest x1 45.8 us: slab_body(): pl.pallas_call(slab_kernel, out_shape=(jax.ShapeDtypeStruct((4, loads, ow...]
    gather x24 -> x2, local copies, waits for them, and re-layouts: 41 us -> 1.83 us  [the longest x1 1.26 us: slab_body(): target = jnp.take(owner_slot[0, 0], member ^ distances, axis=0)]
    all_to_all x2 -> x0, blocking collectives: 25 us -> none  [return_terms(): lax.all_to_all(outgoing, 'grp', split_axis=0, concat_axis=0, tiled=True)]
    all_to_all x6 -> x2, starting transfers between devices: 25.5 us -> 5.39 us  [the longest x1 2.81 us: slab_body(): lax.all_to_all(shared, axes, split_axis=0, concat_axis=0, tiled=True)]
    ppermute x0 -> x6, starting transfers between devices: none -> 10.8 us  [swapped(): lax.ppermute(array, 'grp', [(i, i ^ distance) for i in range(PLACES)])]
  transfers between devices with their start and end apart: 6 -> 8, of which waited for: 5 -> 3; matrix products, arithmetic and copies ran while one was open for 4% -> 9% of each run, Pallas kernels for 0% -> 0%
where the time goes in v1:
time: 123 us; the launch traced here: 122 us
  Pallas kernels  47.4 us (39%)
  waiting for transfers between devices  35 us (28%)
  local copies, waits for them, and re-layouts  17.4 us (14%)
  starting transfers between devices  16.2 us (13%)
  other arithmetic  4.63 us (4%)
  between operations  1.48 us (1%)
    pallas_call x1, Pallas kernels, slab_body(): pl.pallas_call(slab_kernel, out_shape=(jax.ShapeDtypeStruct((4, loads, ow...  45.8 us
    all_to_all x1, waiting for transfers between devices, slab_body(): lax.all_to_all(shared, axes, split_axis=0, concat_axis=0, tiled=True)  18.4 us
    ppermute x6, starting transfers between devices, swapped(): lax.ppermute(array, 'grp', [(i, i ^ distance) for i in range(PLACES)])  10.8 us
    all_to_all x1, waiting for transfers between devices, slab_body(): lax.all_to_all(jnp.broadcast_to(gram[None], (devices, 8, LANES)), axes, 0...  8.37 us
    ppermute x6, waiting for transfers between devices, swapped(): lax.ppermute(array, 'grp', [(i, i ^ distance) for i in range(PLACES)])  8.25 us
    unnamed x37, local copies, waits for them, and re-layouts  7.28 us
    all_to_all x1, starting transfers between devices, slab_body(): lax.all_to_all(shared, axes, split_axis=0, concat_axis=0, tiled=True)  2.81 us
    unnamed x3, other arithmetic  2.73 us
  transfers between devices with their start and end apart: 8, of which 3 were waited for; matrix products, arithmetic and copies ran while one was open for 9% of the time, Pallas kernels for 0%

profile of v1, /device:TPU:0, one launch (start us, length us, event | category | flops | bytes accessed | tf_op | source)
XLA Modules:
  0.0 122.4 jit_solution(2932070400143500800)
XLA Ops:
  1.9 1.3 %gather_fusion.1 = s32[4,316]{1,0:T(4,128)S(1)} fusion(s32[4,316]{1,0:T(4,128)} %bitcast.42, s32[1024]{0:T(1024)S(1)} %pad_clamp_fusion), kind=kCustom, calls=%fused_computation.1.clone | custom fusion | bytes 10128 | tf_op jit(solution)/shard_map/jit(_take)/gather | solution.py:366
  3.2 0.7 reduce.2
  4.5 1.3 %reduce.7 = f32[4]{0:T(128)S(1)} reduce(f32[1,1,4]{2,1,0:T(1,128)} %param.14, f32[]{:T(128)} %broadcast.106), dimensions={0,1}, to_apply=%param.14.reduce_sub_computation.3 | reduce | bytes 36 | tf_op args[3]
  6.1 3.1 %collective-permute-start.3 = (f32[8,768]{1,0:T(8,128)S(1)}, f32[8,768]{1,0:T(8,128)S(1)}, u32[]{:S(2)}, u32[]{:S(2)}) collective-permute-start(f32[8,768]{1,0:T(8,128)S(1)} %fusion.1.t0_ref), channel_id=1, source_target_pairs={{0,1},{1,0},{2,3},{3,2},{4,5},{5,4},{6,7},{7,6},{8,9},{9,8},{10,11... | collective-permute-start | bytes 73736 | tf_op jit(solution)/shard_map/ppermute | solution.py:387
  9.2 2.6 %collective-permute-start.4 = (f32[8,768]{1,0:T(8,128)S(1)}, f32[8,768]{1,0:T(8,128)S(1)}, u32[]{:S(2)}, u32[]{:S(2)}) collective-permute-start(f32[8,768]{1,0:T(8,128)S(1)} %fusion.1.t0_ref), channel_id=1, source_target_pairs={{0,2},{1,3},{2,0},{3,1},{4,6},{5,7},{6,4},{7,5},{8,10},{9,11},{10,... | collective-permute-start | bytes 73736 | tf_op jit(solution)/shard_map/ppermute | solution.py:387
  12.7 1.0 copy.42
  14.4 3.9 %collective-permute-start.2 = (bf16[144,768]{0,1:T(8,128)(2,1)S(1)}, bf16[144,768]{0,1:T(8,128)(2,1)S(1)}, u32[]{:S(2)}, u32[]{:S(2)}) collective-permute-start(bf16[144,768]{0,1:T(8,128)(2,1)S(1)} %maximum_maximum_fusion), channel_id=1, source_target_pairs={{0,3},{1,2},{2,1},{3,0},{4,7},{5,6},{6,5},{7,4},{8,11},{9,10},{10,... | collective-permute-start | bytes 663560 | tf_op jit(solution)/shard_map/ppermute | solution.py:387
  19.3 2.8 %all-to-all-start = ((f32[32,2,128]{2,1,0:T(2,128)}), f32[32,2,128]{2,1,0:T(2,128)S(1)}, u32[]{:S(2)}, u32[]{:S(2)}) async-start(f32[32,2,128]{2,1,0:T(2,128)} %broadcast_in_dim.56), calls=%async_computation | async-start | bytes 65536 | tf_op jit(solution)/shard_map/all_to_all | solution.py:391
  22.3 0.9 pad_maximum_fusion.matrices_ref
  23.3 8.2 %collective-permute-done = bf16[144,768]{0,1:T(8,128)(2,1)S(1)} collective-permute-done((bf16[144,768]{0,1:T(8,128)(2,1)S(1)}, bf16[144,768]{0,1:T(8,128)(2,1)S(1)}, u32[]{:S(2)}, u32[]{:S(2)}) %collective-permute-start) | collective-permute-done | bytes 221216 | tf_op jit(solution)/shard_map/ppermute | solution.py:387
  32.8 0.8 copy.27.x0_ref
  35.5 18.4 %all-to-all-done = f32[32,2,128]{2,1,0:T(2,128)S(1)} async-done(((f32[32,2,128]{2,1,0:T(2,128)}), f32[32,2,128]{2,1,0:T(2,128)S(1)}, u32[]{:S(2)}, u32[]{:S(2)}) %all-to-all-start) | async-done | bytes 32800 | tf_op jit(solution)/shard_map/all_to_all | solution.py:391
  55.1 0.8 copy.28.x1_ref
  55.9 0.8 copy.29.x2_ref
  56.8 0.8 copy.30.x3_ref
  58.3 45.8 %slab.1 = (f32[4,128,768]{2,1,0:T(8,128)}, f32[8,768]{1,0:T(8,128)}, f32[8,128]{1,0:T(8,128)}) custom-call(s32[8]{0:T(128)} %stack.35.order_ref, bf16[144,768]{1,0:T(8,128)(2,1)} %copy.27.x0_ref, bf16[144,768]{1,0:T(8,128)(2,1)} %copy.28.x1_ref, bf16[144,768]{1,0:T(8,128)(2,1)} %copy.29.x2_ref, bf16[144,768]{1,0:T(8,128)(2,1)} %copy.30.x3_ref, ...), custom_call_target="tpu_custom_call" | custom-call | tf_op jit(solution)/shard_map/slab/pallas_call | solution.py:401
  104.1 1.3 %broadcast_in_dim.58 = f32[32,8,128]{2,1,0:T(8,128)} broadcast(f32[8,128]{1,0:T(8,128)} %get-tuple-element.8), dimensions={1,2} | broadcast | bytes 135168 | tf_op jit(solution)/shard_map/broadcast_in_dim | solution.py:429
  105.4 2.6 %all-to-all-start.1 = ((f32[32,8,128]{2,1,0:T(8,128)}), f32[32,8,128]{2,1,0:T(8,128)S(1)}, u32[]{:S(2)}, u32[]{:S(2)}) async-start(f32[32,8,128]{2,1,0:T(8,128)} %broadcast_in_dim.58), calls=%async_computation.1 | async-start | bytes 262144 | tf_op jit(solution)/shard_map/all_to_all | solution.py:428
  108.1 8.4 %all-to-all-done.1.gram_ref = f32[32,8,128]{2,1,0:T(8,128)S(1)} async-done(((f32[32,8,128]{2,1,0:T(8,128)}), f32[32,8,128]{2,1,0:T(8,128)S(1)}, u32[]{:S(2)}, u32[]{:S(2)}) %all-to-all-start.1) | async-done | bytes 131104 | tf_op jit(solution)/shard_map/all_to_all | solution.py:428
  116.5 1.4 %copy-done.1 = f32[4,128,768]{2,1,0:T(8,128)S(1)} copy-done((f32[4,128,768]{2,1,0:T(8,128)S(1)}, f32[4,128,768]{2,1,0:T(8,128)}, u32[]{:S(2)}) %copy-start.1) | copy-done | bytes 1572888
  117.9 0.7 copy-done.4
  118.6 1.5 %finish.1 = (f32[750,128]{1,0:T(8,128)S(1)}, f32[750,128]{1,0:T(8,128)S(1)}) custom-call(s32[8]{0:T(128)S(1)} %copy-done.5, f32[32,8,128]{2,1,0:T(8,128)S(1)} %all-to-all-done.1.gram_ref, f32[32,32]{1,0:T(8,128)S(1)} %bitcast.40, f32[4,128,768]{2,1,0:T(8,128)S(1)} %copy-done.1, f32[8,768]{1,0:T(8,128)S(1)} %copy-done.4, f32[1,768]{1,0:T(1,128)S(1)} %copy-done.3, ...), custom_call_target="tpu_custom_call" | custom-call | tf_op jit(solution)/shard_map/finish/pallas_call | solution.py:431
  120.1 1.1 copy.31
  121.2 1.1 copy.32
  (69 shorter events, 9.2 us)
Async XLA Ops:
  0.6 0.7 copy-start
  0.6 17.7 %copy-start.13 = (f32[1,1,750]{2,1,0:T(1,128)S(1)}, f32[1,1,750]{2,1,0:T(1,128)}, u32[]{:S(2)}) copy-start(f32[1,1,750]{2,1,0:T(1,128)} %param.15) | copy-start | bytes 9004
  0.7 17.7 %copy-start.6 = (f32[1,1,750,128]{3,1,2,0:T(1,128)S(1)}, f32[1,1,750,128]{3,1,2,0:T(1,128)}, u32[]{:S(2)}) copy-start(f32[1,1,750,128]{3,1,2,0:T(1,128)} %param.11) | copy-start | bytes 1152004
  0.7 18.0 %copy-start.14 = (f32[1,32]{1,0:T(1,128)S(1)}, f32[1,32]{1,0:T(1,128)}, u32[]{:S(2)}) copy-start(f32[1,32]{1,0:T(1,128)} %param.16) | copy-start | bytes 388
  0.7 21.5 %copy-start.8 = (bf16[375,375]{1,0:T(8,128)(2,1)S(1)}, bf16[375,375]{1,0:T(8,128)(2,1)}, u32[]{:S(2)}) copy-start(bf16[375,375]{1,0:T(8,128)(2,1)} %param.12) | copy-start | bytes 843754
  0.7 21.5 %copy-start.7 = (bf16[375,375]{1,0:T(8,128)(2,1)S(1)}, bf16[375,375]{1,0:T(8,128)(2,1)}, u32[]{:S(2)}) copy-start(bf16[375,375]{1,0:T(8,128)(2,1)} %param.13) | copy-start | bytes 843754
  6.1 25.4 %copy-start.9 = (f32[8,768]{1,0:T(8,128)}, f32[8,768]{1,0:T(8,128)S(1)}, u32[]{:S(2)}) copy-start(f32[8,768]{1,0:T(8,128)S(1)} %fusion.1.t0_ref) | copy-start | bytes 73732
  6.1 51.5 %collective-permute-start.3 = (f32[8,768]{1,0:T(8,128)S(1)}, f32[8,768]{1,0:T(8,128)S(1)}, u32[]{:S(2)}, u32[]{:S(2)}) collective-permute-start(f32[8,768]{1,0:T(8,128)S(1)} %fusion.1.t0_ref), channel_id=1, source_target_pairs={{0,1},{1,0},{2,3},{3,2},{4,5},{5,4},{6,7},{7,6},{8,9},{9,8},{10,11... | collective-permute-start | bytes 73736 | tf_op jit(solution)/shard_map/ppermute | solution.py:387
  9.2 48.4 %collective-permute-start.4 = (f32[8,768]{1,0:T(8,128)S(1)}, f32[8,768]{1,0:T(8,128)S(1)}, u32[]{:S(2)}, u32[]{:S(2)}) collective-permute-start(f32[8,768]{1,0:T(8,128)S(1)} %fusion.1.t0_ref), channel_id=1, source_target_pairs={{0,2},{1,3},{2,0},{3,1},{4,6},{5,7},{6,4},{7,5},{8,10},{9,11},{10,... | collective-permute-start | bytes 73736 | tf_op jit(solution)/shard_map/ppermute | solution.py:387
  13.9 17.6 %collective-permute-start = (bf16[144,768]{0,1:T(8,128)(2,1)S(1)}, bf16[144,768]{0,1:T(8,128)(2,1)S(1)}, u32[]{:S(2)}, u32[]{:S(2)}) collective-permute-start(bf16[144,768]{0,1:T(8,128)(2,1)S(1)} %maximum_maximum_fusion), channel_id=1, source_target_pairs={{0,1},{1,0},{2,3},{3,2},{4,5},{5,4},{6,7},{7,6},{8,9},{9,8},{10,11... | collective-permute-start | bytes 663560 | tf_op jit(solution)/shard_map/ppermute | solution.py:387
  14.4 41.5 %collective-permute-start.1 = (bf16[144,768]{0,1:T(8,128)(2,1)S(1)}, bf16[144,768]{0,1:T(8,128)(2,1)S(1)}, u32[]{:S(2)}, u32[]{:S(2)}) collective-permute-start(bf16[144,768]{0,1:T(8,128)(2,1)S(1)} %maximum_maximum_fusion), channel_id=1, source_target_pairs={{0,2},{1,3},{2,0},{3,1},{4,6},{5,7},{6,4},{7,5},{8,10},{9,11},{10,... | collective-permute-start | bytes 663560 | tf_op jit(solution)/shard_map/ppermute | solution.py:387
  14.4 42.4 %collective-permute-start.2 = (bf16[144,768]{0,1:T(8,128)(2,1)S(1)}, bf16[144,768]{0,1:T(8,128)(2,1)S(1)}, u32[]{:S(2)}, u32[]{:S(2)}) collective-permute-start(bf16[144,768]{0,1:T(8,128)(2,1)S(1)} %maximum_maximum_fusion), channel_id=1, source_target_pairs={{0,3},{1,2},{2,1},{3,0},{4,7},{5,6},{6,5},{7,4},{8,11},{9,10},{10,... | collective-permute-start | bytes 663560 | tf_op jit(solution)/shard_map/ppermute | solution.py:387
  19.3 34.5 %all-to-all-start = ((f32[32,2,128]{2,1,0:T(2,128)}), f32[32,2,128]{2,1,0:T(2,128)S(1)}, u32[]{:S(2)}, u32[]{:S(2)}) async-start(f32[32,2,128]{2,1,0:T(2,128)} %broadcast_in_dim.56), calls=%async_computation | async-start | bytes 65536 | tf_op jit(solution)/shard_map/all_to_all | solution.py:391
  31.5 26.1 %collective-permute-start.5 = (f32[8,768]{1,0:T(8,128)S(1)}, f32[8,768]{1,0:T(8,128)S(1)}, u32[]{:S(2)}, u32[]{:S(2)}) collective-permute-start(f32[8,768]{1,0:T(8,128)S(1)} %fusion.1.t0_ref), channel_id=1, source_target_pairs={{0,3},{1,2},{2,1},{3,0},{4,7},{5,6},{6,5},{7,4},{8,11},{9,10},{10,... | collective-permute-start | bytes 73736 | tf_op jit(solution)/shard_map/ppermute | solution.py:387
  56.8 59.7 %copy-start.2 = (f32[32,1,32]{2,1,0:T(1,128)S(1)}, f32[32,1,32]{2,1,0:T(1,128)}, u32[]{:S(2)}) copy-start(f32[32,1,32]{2,1,0:T(1,128)} %slice.18) | copy-start | bytes 12292
  56.8 59.7 %copy-start.3 = (f32[1,768]{1,0:T(1,128)S(1)}, f32[1,768]{1,0:T(1,128)}, u32[]{:S(2)}) copy-start(f32[1,768]{1,0:T(1,128)} %broadcast_in_dim.57.basis_ref) | copy-start | bytes 9220
  56.8 59.7 %copy-start.5 = (s32[8]{0:T(128)S(1)}, s32[8]{0:T(128)}, u32[]{:S(2)}) copy-start(s32[8]{0:T(128)} %stack.35.order_ref) | copy-start | bytes 100
  57.6 0.6 copy-start.10
  57.6 0.6 copy-start.11
  57.7 0.6 copy-start.12
  105.4 11.0 %all-to-all-start.1 = ((f32[32,8,128]{2,1,0:T(8,128)}), f32[32,8,128]{2,1,0:T(8,128)S(1)}, u32[]{:S(2)}, u32[]{:S(2)}) async-start(f32[32,8,128]{2,1,0:T(8,128)} %broadcast_in_dim.58), calls=%async_computation.1 | async-start | bytes 262144 | tf_op jit(solution)/shard_map/all_to_all | solution.py:428
  116.4 1.4 %copy-start.1 = (f32[4,128,768]{2,1,0:T(8,128)S(1)}, f32[4,128,768]{2,1,0:T(8,128)}, u32[]{:S(2)}) copy-start(f32[4,128,768]{2,1,0:T(8,128)} %get-tuple-element.9.fields_ref) | copy-start | bytes 4718596
  117.9 0.7 copy-start.4

commit v2 on v0

--- a/solution.py
+++ b/solution.py
@@ -1,9 +1,623 @@
+import functools
+
 import jax
 import jax.numpy as jnp
 from jax import lax
+from jax.experimental import pallas as pl
+from jax.experimental.pallas import tpu as pltpu
 from jax.sharding import PartitionSpec as P
 
 ITERS = 2
+LANES = 128
+RIDERS = 16
+PLACES = 4
+
+
+def round_up(value, unit):
+    return -(-value // unit) * unit
+
+
+def place_distances(order_ref):
+    return [0] + [order_ref[place - 1] for place in range(1, PLACES)]
+
+
+def turn(ref, rows, width):
+    return ref[rows : rows + LANES, :width].T
+
+
+def pack_kernel(
+    forces_hbm,
+    basis_hbm,
+    inverse_hbm,
+    send_hbm,
+    owner_hbm,
+    home_hbm,
+    moduli_hbm,
+    packed_ref,
+    table_ref,
+    padded,
+    wide_ref,
+    basis_ref,
+    inverse_ref,
+    send_ref,
+    owner_ref,
+    home_ref,
+    moduli_ref,
+    square,
+    arrived,
+):
+    f32, bf16 = jnp.float32, jnp.bfloat16
+    owned, _, loads = forces_hbm.shape
+    wide = padded.shape[0]
+    half = table_ref.shape[1]
+    members, capacity = send_ref.shape
+    local = home_ref.shape[1]
+    copies = [
+        pltpu.make_async_copy(source, target, arrived.at[at])
+        for at, (source, target) in enumerate(
+            (
+                (forces_hbm.at[:, 0, :], padded.at[:owned, :]),
+                (basis_hbm, basis_ref),
+                (inverse_hbm, inverse_ref),
+                (send_hbm, send_ref),
+                (owner_hbm, owner_ref),
+                (home_hbm, home_ref),
+                (moduli_hbm, moduli_ref),
+            )
+        )
+    ]
+    for copy in copies:
+        copy.start()
+    padded[owned:, :] = jnp.zeros((wide - owned, loads), f32)
+    wide_ref[...] = jnp.zeros_like(wide_ref)
+    table_ref[...] = jnp.full(table_ref.shape, -1.0, f32)
+    for copy in copies:
+        copy.wait()
+    wide_ref[0:1, :owned] = basis_ref[...]
+    basis = wide_ref[0:1, :]
+    term = jnp.zeros((loads, 1), f32)
+    for start in range(0, wide, LANES):
+        turned = padded[start : start + LANES, :].T
+        packed_ref[:loads, start : start + LANES] = turned.astype(bf16)
+        term = term + jnp.sum(
+            turned * basis[:, start : start + LANES], axis=1, keepdims=True
+        )
+    row_ids = lax.broadcasted_iota(jnp.int32, (RIDERS, wide), 0)
+    packed_ref[loads:, :] = jnp.where(row_ids == 0, basis, 0.0).astype(bf16)
+
+    table_ref[0:1, :] = home_ref[:, :half].astype(f32)
+    table_ref[1:2, : local - half] = home_ref[:, half:].astype(f32)
+    table_ref[2 : 2 + members, :capacity] = send_ref[...].astype(f32)
+    table_ref[2 : 2 + members, half // 2 : half // 2 + capacity] = owner_ref[...].astype(f32)
+    table_ref[6:7, : moduli_ref.shape[1]] = moduli_ref[...]
+    square[...] = jnp.broadcast_to(term, square.shape)
+    table_ref[7:8, :] = jnp.zeros((1, half), f32)
+    table_ref[7:8, :LANES] = square[...].T[0:1, :]
+    table_ref[7:8, LANES : LANES + inverse_ref.shape[1]] = inverse_ref[...]
+
+
+def build_kernel(
+    size,
+    owned_count,
+    local_count,
+    order_ref,
+    tables,
+    pick0,
+    pick1,
+    pick2,
+    pick3,
+    put0,
+    put1,
+    put2,
+    put3,
+    factors,
+    slots,
+    homes,
+    sources,
+    sources_t,
+):
+    picks, puts = (pick0, pick1, pick2, pick3), (put0, put1, put2, put3)
+    owned, half = pick0.shape[1], pick0.shape[2]
+    block = half // 2
+    slot_count = slots.shape[1]
+    f32, bf16 = jnp.float32, jnp.bfloat16
+    distance = place_distances(order_ref)
+    member = order_ref[3]
+    elements = 4
+    sources[...] = jnp.full(sources.shape, -1.0, f32)
+    slots[...] = jnp.full(slots.shape, -1.0, f32)
+    homes[...] = jnp.zeros_like(homes)
+    lane_block = lax.broadcasted_iota(jnp.int32, (8, block), 1)
+    for place in range(PLACES):
+        homes[place : place + 1, :half] = tables[distance[place], 0:1, :]
+        homes[place : place + 1, half:] = tables[distance[place], 1:2, :]
+        for e in range(elements):
+            modulus = jnp.broadcast_to(tables[distance[place], 6:7, e : e + 1], (1, block))
+            factors[0, place, e : e + 1, :] = modulus
+            factors[1, place, e : e + 1, :] = 1.0 / modulus
+
+    all_homes = homes[...]
+    for e in range(elements):
+        shift = (all_homes.shape[1] - e * size) % all_homes.shape[1]
+        moved = all_homes if e == 0 else pltpu.roll(all_homes, shift, 1)
+        rows = moved[:, :block]
+        rows = jnp.where((lane_block < size) & (rows < float(owned_count)), rows, -1.0)
+        part, column = e // 2, (e % 2) * block
+        sources[part * PLACES : (part + 1) * PLACES, column : column + block] = rows[:PLACES]
+
+    pairs = [(a, (a + step) % PLACES) for step in (1, PLACES - 1) for a in range(PLACES)]
+    for pair, (reader, owner) in enumerate(pairs):
+        to_owner = pl.ds(2 + (member ^ distance[owner]), 1)
+        to_reader = pl.ds(2 + (member ^ distance[reader]), 1)
+        sent = tables[distance[reader], to_owner, :slot_count]
+        sent = jnp.where(sent < float(local_count), sent, -1.0)
+        first = float(2 * size)
+        moved = sent - first + jnp.where(sent >= first + size, float(block - size), 0.0)
+        slots[2 * pair : 2 * pair + 1, :] = jnp.where(sent < 0.0, -1.0, moved)
+        slots[2 * pair + 1 : 2 * pair + 2, :] = tables[distance[owner], to_reader, slot_count:]
+    slots_t = slots[...].T
+    half_ids = lax.broadcasted_iota(jnp.int32, (LANES, half), 1).astype(f32)
+    for pair in range(len(pairs)):
+        found = jnp.zeros((1, half), f32)
+        for start in range(0, slot_count, LANES):
+            column = slots_t[start : start + LANES, 2 * pair : 2 * pair + 1]
+            target = slots_t[start : start + LANES, 2 * pair + 1 : 2 * pair + 2] + 1.0
+            found = found + jnp.sum(
+                jnp.where(half_ids == column, target, 0.0), axis=0, keepdims=True
+            )
+        sources[2 * PLACES + pair : 2 * PLACES + pair + 1, :] = found - 1.0
+    sources_t[...] = sources[...].T
+
+    chunk = 256
+    lane_ids = lax.broadcasted_iota(jnp.int32, (chunk, owned), 1).astype(f32)
+    deep_ids = lax.broadcasted_iota(jnp.int32, (chunk, half), 0).astype(f32)
+    column_ids = lax.broadcasted_iota(jnp.int32, (chunk, LANES), 1)
+
+    for kind, (pick, put) in enumerate(zip(picks, puts)):
+
+        def build(place, carry):
+            n = kind * PLACES + place
+            source = sources[pl.ds(n, 1), :]
+            for start in range(0, owned, chunk):
+                pick[place, start : start + chunk, :] = jnp.where(
+                    deep_ids == source - float(start), 1.0, 0.0
+                ).astype(bf16)
+            for start in range(0, half, chunk):
+                column = jnp.sum(
+                    jnp.where(column_ids == n, sources_t[start : start + chunk, :], 0.0),
+                    axis=1,
+                    keepdims=True,
+                )
+                put[place, start : start + chunk, :] = jnp.where(
+                    lane_ids == column, 1.0, 0.0
+                ).astype(bf16)
+            return carry
+
+        lax.fori_loop(0, PLACES, build, 0)
+
+
+def chain_kernel(
+    order_ref,
+    x0_ref,
+    x1_ref,
+    x2_ref,
+    x3_ref,
+    pick0,
+    pick1,
+    pick2,
+    pick3,
+    put0,
+    put1,
+    put2,
+    put3,
+    factors,
+    matrices_ref,
+    own,
+    values,
+    terms,
+    copies,
+    riders,
+):
+    owned, half = pick0.shape[1], pick0.shape[2]
+    block = matrices_ref.shape[1]
+    rows = own.shape[1]
+    loads = rows - RIDERS
+    f32, bf16 = jnp.float32, jnp.bfloat16
+    distance = place_distances(order_ref)
+    for at, x_ref in enumerate((x0_ref, x1_ref, x2_ref, x3_ref)):
+        values[1, at] = x_ref[...]
+    row_ids = lax.broadcasted_iota(jnp.int32, (RIDERS, owned), 0)
+    for place in range(PLACES):
+        values[0, place] = values[1, distance[place]]
+        riders[place] = jnp.where(
+            row_ids == place, values[0, place, loads : loads + 1, :].astype(f32), 0.0
+        ).astype(bf16)
+
+    def multiply(left, right):
+        return jnp.dot(left, right, preferred_element_type=f32)
+
+    def beside(refs):
+        return jnp.concatenate(refs, axis=1)
+
+    def above(refs):
+        return jnp.concatenate(refs, axis=0)
+
+    def split(place, part, copied):
+        copied = copied.astype(bf16)
+        copies[place, 2 * part] = copied[:, :block]
+        copies[place, 2 * part + 1] = copied[:, block:]
+
+    def inner(source, place):
+        split(place, 0, multiply(values[source, place], pick0[place]))
+
+    def outer(source, place):
+        ahead, behind = (place + 1) % PLACES, (place - 1) % PLACES
+        fields = beside([values[source, at] for at in (place, ahead, behind)])
+        split(place, 1, multiply(fields, above([pick1[place], pick2[place], pick3[place]])))
+
+    def scaled(which, at, count):
+        product = multiply(copies[at].reshape(count * 4 * rows, block), matrices_ref[which])
+        scale = factors[which, at].reshape(count, 4, 1, block)
+        terms[at] = (product.reshape(count, 4, rows, block) * scale).astype(bf16)
+
+    def collect(place):
+        ahead, behind = (place + 1) % PLACES, (place - 1) % PLACES
+        ends = beside(
+            [terms[place, e] for e in range(4)]
+            + [terms[behind, 2], terms[behind, 3], terms[ahead, 2], terms[ahead, 3]]
+        )
+        return multiply(ends, above([put0[place], put1[place], put2[behind], put3[ahead]]))
+
+    def stage(at, carry):
+        which = lax.rem(at + 1, 2)
+        source, target = lax.rem(at, 2), lax.rem(at + 1, 2)
+        for place in range(PLACES):
+            inner(source, place)
+            outer(source, place)
+        scaled(which, slice(0, PLACES), PLACES)
+        for place in range(PLACES):
+            summed = collect(place)
+            values[target, place] = summed.astype(bf16)
+            if place == 0:
+                own[at] = summed
+
+        @pl.when(at == 0)
+        def _():
+            for place in range(PLACES):
+                values[1, place, loads:, :] = riders[place]
+
+        return carry
+
+    lax.fori_loop(0, 3, stage, 0)
+    inner(1, 0)
+    outer(1, 0)
+    outer(1, 1)
+    outer(1, 3)
+    scaled(0, slice(0, 2), 2)
+    scaled(0, slice(3, 4), 1)
+    own[3] = collect(0)
+
+
+def dots_kernel(
+    order_ref,
+    own,
+    x0_ref,
+    shared_ref,
+    wide_ref,
+    fields_ref,
+    gram_ref,
+    inverse,
+    coarse_ref,
+    square,
+):
+    f32 = jnp.float32
+    devices = inverse.shape[0]
+    loads = fields_ref.shape[1]
+    distance = place_distances(order_ref)
+    member = order_ref[3]
+    first = order_ref[4] * PLACES
+    for at in range(devices // PLACES):
+        for apart in range(PLACES):
+            row = pl.ds(at * PLACES + (member ^ apart), 1)
+            coarse_ref[row, :] = shared_ref[at, apart : apart + 1, :]
+            inverse[row, :] = shared_ref[at, PLACES + apart : PLACES + apart + 1, :]
+    square[...] = jnp.zeros_like(square)
+    for place in range(PLACES):
+        square[place : place + 1, :] = inverse[pl.ds(first + (member ^ distance[place]), 1), :]
+    answer = jnp.dot(
+        square[0:8, :devices],
+        coarse_ref[...],
+        precision=lax.Precision.HIGHEST,
+        preferred_element_type=f32,
+    )
+    square[...] = jnp.zeros_like(square)
+    square[0:8, :] = answer
+    answer_t = square[...].T
+    basis = wide_ref[0:1, :]
+    start_field = own[0, :loads, :] + answer_t[:, 0:1] * basis
+    start_image = own[1, :loads, :]
+    next_field = own[2, :loads, :]
+    next_image = own[3, :loads, :]
+    for place in range(PLACES):
+        column = answer_t[:, place : place + 1]
+        row = loads + place
+        start_image = start_image + column * own[1, row : row + 1, :]
+        next_field = next_field + column * own[2, row : row + 1, :]
+        next_image = next_image + column * own[3, row : row + 1, :]
+    fields_ref[0] = start_field
+    fields_ref[1] = next_field
+    fields_ref[2] = start_image
+    fields_ref[3] = next_image
+    residual = x0_ref[:loads, :].astype(f32)
+    lanes = lax.broadcasted_iota(jnp.int32, square.shape, 1)
+    collected = jnp.zeros(square.shape, f32)
+    for at, product in enumerate(
+        (
+            residual * start_field,
+            start_field * start_image,
+            start_image * next_field,
+            next_field * next_image,
+            basis * start_image,
+            basis * next_image,
+        )
+    ):
+        total = jnp.sum(product, axis=1, keepdims=True)
+        collected = jnp.where(lanes == at, total, collected)
+    gram = collected.T[0:8, :]
+    row_at = lax.broadcasted_iota(jnp.int32, gram.shape, 0)
+    lane_at = lax.broadcasted_iota(jnp.int32, gram.shape, 1)
+    for place in range(PLACES):
+        entry = jnp.sum(
+            basis * own[1, loads + place : loads + place + 1, :], axis=1, keepdims=True
+        )
+        here = (row_at == 6) & (lane_at == first + (member ^ distance[place]))
+        gram = jnp.where(here, entry, gram)
+    gram_ref[...] = jnp.broadcast_to(gram[None], gram_ref.shape)
+
+
+def finish_kernel(
+    order_ref,
+    gram_ref,
+    inverse,
+    fields_ref,
+    own,
+    wide_ref,
+    padded,
+    solution_hbm,
+    residual_hbm,
+    answer,
+    square,
+    iterates,
+    residuals,
+    sent,
+):
+    f32 = jnp.float32
+    count = inverse.shape[0]
+    owned, _, loads = solution_hbm.shape
+    first = order_ref[4] * PLACES
+    member = order_ref[3]
+    distance = place_distances(order_ref)
+    precise = functools.partial(
+        jnp.dot, precision=lax.Precision.HIGHEST, preferred_element_type=f32
+    )
+    coarse = gram_ref[:, 4, :]
+    answer[...] = precise(inverse[:, :count], coarse)
+    answers = answer[...]
+    mixed = precise(gram_ref[:, 6, :count], answers)
+    sums = jnp.sum(gram_ref[...], axis=0)
+    weighted, curvature = sums[0:1, :], sums[1:2, :]
+    cross = sums[2:3, :] + jnp.sum(coarse * answers, axis=0, keepdims=True)
+    last = sums[3:4, :] + jnp.sum(
+        answers * (2.0 * gram_ref[:, 5, :] + mixed), axis=0, keepdims=True
+    )
+    step = weighted / curvature
+    update = step * step * cross - weighted
+    grown = 1.0 + update / weighted
+    curvature = grown * grown * curvature - 2.0 * step * grown * cross + step * step * last
+    second = update / curvature
+    whole = step + second * grown
+    back = step * second
+    square[...] = jnp.zeros_like(square)
+    square[0:1, :] = whole
+    square[1:2, :] = back
+    for place in range(PLACES):
+        at = first + (member ^ distance[place])
+        square[2 + place : 3 + place, :] = back * answer[pl.ds(at, 1), :]
+    columns = square[...].T
+    whole, back = columns[:, 0:1], columns[:, 1:2]
+    copies = []
+    for start in range(0, wide_ref.shape[1], LANES):
+        part = slice(start, start + LANES)
+        size = min(LANES, owned - start)
+        iterate = (
+            whole * fields_ref[0, :, part]
+            - back * fields_ref[1, :, part]
+            - columns[:, 2:3] * wide_ref[0:1, part]
+        )
+        change = back * fields_ref[3, :, part] - whole * fields_ref[2, :, part]
+        for place in range(PLACES):
+            row = loads + place
+            change = change + columns[:, 2 + place : 3 + place] * own[1, row : row + 1, part]
+        iterates[start : start + LANES, :] = iterate.T
+        residuals[start : start + LANES, :] = padded[start : start + LANES, :] + change.T
+        rows = slice(start, start + size)
+        for at, (source, target) in enumerate(
+            ((iterates, solution_hbm), (residuals, residual_hbm))
+        ):
+            copy = pltpu.make_async_copy(
+                source.at[rows, :], target.at[rows, 0, :], sent.at[at, start // LANES]
+            )
+            copy.start()
+            copies.append(copy)
+    for copy in copies:
+        copy.wait()
+
+
+def slab_body(
+    mesh_shape,
+    forces,
+    stiffness,
+    local_solve,
+    moduli,
+    coarse_basis,
+    coarse_inverse,
+    send_index,
+    owner_slot,
+    home_slot,
+):
+    f32, bf16, i32 = jnp.float32, jnp.bfloat16, jnp.int32
+    axes = ("sub", "grp")
+    owned_count, loads = forces.shape[2:]
+    size = stiffness.shape[0]
+    local_count = home_slot.shape[2]
+    owned_wide = round_up(owned_count, 256)
+    block = round_up(size, LANES)
+    half = 2 * block
+    devices = mesh_shape["sub"] * mesh_shape["grp"]
+    rows = loads + RIDERS
+    slab = lax.axis_index("sub")
+    member = lax.axis_index("grp")
+    smem = pl.BlockSpec(memory_space=pltpu.SMEM)
+    vmem = pl.BlockSpec(memory_space=pltpu.VMEM)
+
+    anywhere = pl.BlockSpec(memory_space=pltpu.HBM)
+    slabs = mesh_shape["sub"]
+
+    packed, table, padded, wide = pl.pallas_call(
+        pack_kernel,
+        out_shape=(
+            jax.ShapeDtypeStruct((rows, owned_wide), bf16),
+            jax.ShapeDtypeStruct((8, half), f32),
+            jax.ShapeDtypeStruct((owned_wide, loads), f32),
+            jax.ShapeDtypeStruct((8, owned_wide), f32),
+        ),
+        in_specs=[anywhere] * 7,
+        out_specs=(vmem,) * 4,
+        scratch_shapes=[
+            pltpu.VMEM((1, owned_count), f32),
+            pltpu.VMEM((1, devices), f32),
+            pltpu.VMEM(send_index.shape[2:], i32),
+            pltpu.VMEM(owner_slot.shape[2:], i32),
+            pltpu.VMEM((1, local_count), i32),
+            pltpu.VMEM((1, moduli.shape[2]), f32),
+            pltpu.VMEM((LANES, LANES), f32),
+            pltpu.SemaphoreType.DMA((7,)),
+        ],
+        compiler_params=pltpu.CompilerParams(vmem_limit_bytes=62 * 2**20),
+        name="pack",
+    )(
+        forces.reshape(owned_count, 1, loads),
+        coarse_basis[0],
+        coarse_inverse,
+        send_index[0, 0],
+        owner_slot[0, 0],
+        home_slot[0],
+        moduli[0],
+    )
+
+    used = send_index[0, 0, :, 0] < local_count
+    distances = jnp.arange(PLACES, dtype=i32) ^ member
+    opposite = jnp.clip(jnp.sum(jnp.where(used, 0, distances)), 1, PLACES - 1)
+    near = jnp.where(opposite == 1, 2, 1)
+    order = jnp.stack(
+        [
+            near,
+            opposite,
+            6 - near - opposite,
+            member,
+            slab,
+            slab,
+            slab,
+            slab,
+        ]
+    ).astype(i32)
+
+    def swapped(array, distance):
+        return lax.ppermute(array, "grp", [(i, i ^ distance) for i in range(PLACES)])
+
+    near_table = swapped(table, 1)
+    packed, near_table = lax.optimization_barrier((packed, near_table))
+    tables = jnp.stack([table, near_table, swapped(table, 2), swapped(table, 3)])
+    fields = [packed] + [swapped(packed, d) for d in range(1, PLACES)]
+    shared = jnp.concatenate([tables[:, 7, :LANES], tables[:, 7, LANES : 2 * LANES]], axis=0)
+    shared = jnp.broadcast_to(shared[None], (slabs, 8, LANES))
+    shared = lax.all_to_all(shared, "sub", split_axis=0, concat_axis=0, tiled=True)
+
+    widen = ((0, block - size), (0, block - size))
+    matrices = jnp.stack([jnp.pad(stiffness, widen), jnp.pad(local_solve, widen)])
+
+    *choices, factors = pl.pallas_call(
+        functools.partial(build_kernel, size, owned_count, local_count),
+        out_shape=(
+            *[jax.ShapeDtypeStruct((PLACES, owned_wide, half), bf16)] * 4,
+            *[jax.ShapeDtypeStruct((PLACES, half, owned_wide), bf16)] * 4,
+            jax.ShapeDtypeStruct((2, PLACES, 4, block), f32),
+        ),
+        in_specs=[smem, vmem],
+        out_specs=(vmem,) * 9,
+        scratch_shapes=[
+            pltpu.VMEM((LANES, half // 2), f32),
+            pltpu.VMEM((8, 2 * half), f32),
+            pltpu.VMEM((LANES, half), f32),
+            pltpu.VMEM((half, LANES), f32),
+        ],
+        compiler_params=pltpu.CompilerParams(vmem_limit_bytes=8 * 2**20),
+        cost_estimate=pl.CostEstimate(
+            flops=8 * 10**9, bytes_accessed=38 * 10**6, transcendentals=0
+        ),
+        name="build",
+    )(order, tables)
+
+    own = pl.pallas_call(
+        chain_kernel,
+        out_shape=jax.ShapeDtypeStruct((4, rows, owned_wide), f32),
+        in_specs=[smem] + [vmem] * 14,
+        out_specs=vmem,
+        scratch_shapes=[
+            pltpu.VMEM((2, PLACES, rows, owned_wide), bf16),
+            pltpu.VMEM((PLACES, 4, rows, block), bf16),
+            pltpu.VMEM((PLACES, 4, rows, block), bf16),
+            pltpu.VMEM((PLACES, RIDERS, owned_wide), bf16),
+        ],
+        compiler_params=pltpu.CompilerParams(vmem_limit_bytes=14 * 2**20),
+        cost_estimate=pl.CostEstimate(
+            flops=35 * 10**9, bytes_accessed=38 * 10**6, transcendentals=0
+        ),
+        name="chain",
+    )(order, *fields, *choices, factors, matrices)
+
+
+    results, gram, inverse = pl.pallas_call(
+        dots_kernel,
+        out_shape=(
+            jax.ShapeDtypeStruct((4, loads, owned_wide), f32),
+            jax.ShapeDtypeStruct((devices, 8, LANES), f32),
+            jax.ShapeDtypeStruct((devices, LANES), f32),
+        ),
+        in_specs=[smem] + [vmem] * 4,
+        out_specs=(vmem,) * 3,
+        scratch_shapes=[pltpu.VMEM((devices, LANES), f32), pltpu.VMEM((LANES, LANES), f32)],
+        compiler_params=pltpu.CompilerParams(vmem_limit_bytes=8 * 2**20),
+        name="dots",
+    )(order, own, packed, shared, wide)
+
+    gathered = lax.all_to_all(gram, axes, split_axis=0, concat_axis=0, tiled=True)
+    iterate, residual = pl.pallas_call(
+        finish_kernel,
+        out_shape=(jax.ShapeDtypeStruct((owned_count, 1, loads), f32),) * 2,
+        in_specs=[smem] + [vmem] * 6,
+        out_specs=(anywhere, anywhere),
+        scratch_shapes=[
+            pltpu.VMEM((devices, LANES), f32),
+            pltpu.VMEM((LANES, LANES), f32),
+            pltpu.VMEM((owned_wide, loads), f32),
+            pltpu.VMEM((owned_wide, loads), f32),
+            pltpu.SemaphoreType.DMA((2, owned_wide // LANES)),
+        ],
+        compiler_params=pltpu.CompilerParams(vmem_limit_bytes=8 * 2**20),
+        name="finish",
+    )(order, gathered, inverse, results, own, wide, padded)
+    return (iterate.reshape(forces.shape), residual.reshape(forces.shape))
 
 
 def spread_owned(values, slot_rows):
@@ -22,7 +636,7 @@
     return scaled.astype(jnp.bfloat16).reshape(-1, columns)
 
 
-def body(
+def exchange_body(
     forces,
     stiffness,
     local_solve,
@@ -133,6 +747,10 @@
 
 
 def solution(mesh):
+    if mesh.shape["grp"] == PLACES:
+        body = functools.partial(slab_body, dict(mesh.shape))
+    else:
+        body = exchange_body
     return jax.shard_map(
         body,
         mesh=mesh,

time: 453 us -> 78.9 us (0.17)
  blocking collectives: 246 us -> 12.8 us
  other arithmetic: 83 us -> 2.29 us
  local copies, waits for them, and re-layouts: 64.7 us -> 3.45 us
  Pallas kernels: 0 us -> 41.7 us
  waiting for transfers between devices: 28.5 us -> 2.65 us
  starting transfers between devices: 25.5 us -> 14.1 us
    psum x4 -> x0, blocking collectives: 154 us -> none  [the longest x3 115 us: coarse_step(): lax.psum((spread, jnp.sum(residual * local_part, axis=0)), ('sub', 'grp'))]
    scatter-add x4 -> x0, other arithmetic: 72.5 us -> none  [return_terms(): jnp.zeros((owned_count + 1, columns), jnp.float32).at[gather_rows]]
    all_gather x1 -> x0, blocking collectives: 67 us -> none  [body(): lax.all_gather(coarse_inverse, ('sub', 'grp'), axis=0, tiled=True)]
    pallas_call x0 -> x5, Pallas kernels: none -> 41.7 us  [the longest x1 26.2 us: slab_body(): pl.pallas_call(chain_kernel, out_shape=jax.ShapeDtypeStruct((4, rows, own...]
    gather x24 -> x0, local copies, waits for them, and re-layouts: 41 us -> none  [the longest x8 12.3 us: spread_owned(): return jnp.take(padded, slot_rows, axis=0)]
    all_to_all x6 -> x1, waiting for transfers between devices: 28.5 us -> 0.01 us  [slab_body(): lax.all_to_all(shared, 'sub', split_axis=0, concat_axis=0, tiled=True)]
    all_to_all x6 -> x1, starting transfers between devices: 25.5 us -> 3.87 us  [slab_body(): lax.all_to_all(shared, 'sub', split_axis=0, concat_axis=0, tiled=True)]
    all_to_all x2 -> x1, blocking collectives: 25 us -> 12.8 us  [slab_body(): lax.all_to_all(gram, axes, split_axis=0, concat_axis=0, tiled=True)]
  transfers between devices with their start and end apart: 6 -> 7, of which waited for: 5 -> 1; matrix products, arithmetic and copies ran while one was open for 4% -> 5% of each run, Pallas kernels for 0% -> 46%
where the time goes in v2:
time: 78.9 us; the launch traced here: 78.5 us
  Pallas kernels  41.7 us (53%)
  starting transfers between devices  14.1 us (18%)
  blocking collectives  12.8 us (16%)
  local copies, waits for them, and re-layouts  3.45 us (4%)
  waiting for transfers between devices  2.65 us (3%)
  other arithmetic  2.29 us (3%)
  between operations  1.53 us (2%)
    pallas_call x1, Pallas kernels, slab_body(): pl.pallas_call(chain_kernel, out_shape=jax.ShapeDtypeStruct((4, rows, own...  26.2 us
    all_to_all x1, blocking collectives, slab_body(): lax.all_to_all(gram, axes, split_axis=0, concat_axis=0, tiled=True)  12.8 us
    ppermute x6, starting transfers between devices, swapped(): lax.ppermute(array, 'grp', [(i, i ^ distance) for i in range(PLACES)])  10.2 us
    pallas_call x1, Pallas kernels, slab_body(): pl.pallas_call(functools.partial(build_kernel, size, owned_count, local_c...  9.57 us
    all_to_all x1, starting transfers between devices, slab_body(): lax.all_to_all(shared, 'sub', split_axis=0, concat_axis=0, tiled=True)  3.87 us
    ppermute x6, waiting for transfers between devices, swapped(): lax.ppermute(array, 'grp', [(i, i ^ distance) for i in range(PLACES)])  2.65 us
    pallas_call x1, Pallas kernels, slab_body(): pl.pallas_call(finish_kernel, out_shape=(jax.ShapeDtypeStruct((owned_coun...  2.27 us
    pallas_call x1, Pallas kernels, slab_body(): pl.pallas_call(pack_kernel, out_shape=(jax.ShapeDtypeStruct((rows, owned_...  2.2 us
  transfers between devices with their start and end apart: 7, of which 1 were waited for; matrix products, arithmetic and copies ran while one was open for 5% of the time, Pallas kernels for 46%

profile of v2, /device:TPU:0, one launch (start us, length us, event | category | flops | bytes accessed | tf_op | source)
XLA Modules:
  0.0 78.5 jit_solution(10003357213843933578)
XLA Ops:
  0.6 2.2 %pack.1 = (bf16[144,768]{1,0:T(8,128)(2,1)}, f32[8,768]{1,0:T(8,128)}, f32[768,128]{1,0:T(8,128)}, f32[8,768]{1,0:T(8,128)}) custom-call(f32[750,1,128]{2,1,0:T(1,128)} %bitcast.29, f32[1,750]{1,0:T(1,128)} %bitcast.39, f32[1,32]{1,0:T(1,128)} %inverse_hbm.1, s32[4,316]{1,0:T(4,128)} %bitcast.34, s32[4,316]{1,0:T(4,128)} %bitcast.37, s32[1,1500]{1,0:T(1,128)} %bitcast.38, ...), custom_call_target="tpu_custom_call" | custom-call | tf_op jit(solution)/shard_map/pack/pallas_call | solution.py:486
  2.8 5.1 %collective-permute-start.5 = (f32[8,768]{1,0:T(8,128)}, f32[8,768]{1,0:T(8,128)S(1)}, u32[]{:S(2)}, u32[]{:S(2)}) collective-permute-start(f32[8,768]{1,0:T(8,128)} %get-tuple-element.23), channel_id=1, source_target_pairs={{0,3},{1,2},{2,1},{3,0},{4,7},{5,6},{6,5},{7,4},{8,11},{9,10},{10,... | collective-permute-start | bytes 73736 | tf_op jit(solution)/shard_map/ppermute | solution.py:536
  8.0 0.0 collective-permute-start.4
  8.0 0.6 collective-permute-start
  8.6 0.8 %fusion = pred[4]{0:T(512)(128)(4,1)S(1)} fusion(s32[1,1,4,316]{3,2,1,0:T(4,128)} %param.15), kind=kLoop, calls=%fused_computation.6 | loop fusion | flops 4 | bytes 20 | tf_op jit(solution)/shard_map/lt | solution.py:518
  9.4 1.1 %pad_bitcast_fusion = (bf16[1,384,384]{2,1,0:T(8,128)(2,1)S(1)}, bf16[1,384,384]{2,1,0:T(8,128)(2,1)S(1)}) fusion(bf16[375,375]{1,0:T(8,128)(2,1)} %param.11, bf16[375,375]{1,0:T(8,128)(2,1)} %param.10), kind=kLoop, calls=%fused_computation.1 | loop fusion | bytes 1152324 | tf_op jit(solution)/shard_map/stack | solution.py:547
  10.5 0.1 pad_maximum_fusion.matrices_ref
  10.6 0.7 select_reduce_fusion
  11.9 0.1 stack.50.order_ref
  12.0 0.0 collective-permute-done
  12.0 3.8 %collective-permute-start.3 = (bf16[144,768]{1,0:T(8,128)(2,1)}, bf16[144,768]{1,0:T(8,128)(2,1)S(1)}, u32[]{:S(2)}, u32[]{:S(2)}) collective-permute-start(bf16[144,768]{1,0:T(8,128)(2,1)} %get-tuple-element.24.x0_ref), channel_id=1, source_target_pairs={{0,3},{1,2},{2,1},{3,0},{4,7},{5,6},{6,5},{7,4},{8,11},{9,10},{10,... | collective-permute-start | bytes 663560 | tf_op jit(solution)/shard_map/ppermute | solution.py:536
  15.8 0.6 collective-permute-start.1
  16.4 0.7 pad_maximum_fusion.1.tables
  17.2 0.6 broadcast_in_dim.11
  17.8 3.9 %all-to-all-start = ((f32[8,8,128]{2,1,0:T(8,128)}), f32[8,8,128]{2,1,0:T(8,128)S(1)}, u32[]{:S(2)}, u32[]{:S(2)}) async-start(f32[8,8,128]{2,1,0:T(8,128)} %broadcast_in_dim.11), calls=%async_computation | async-start | bytes 65536 | tf_op jit(solution)/shard_map/all_to_all | solution.py:544
  21.7 9.6 %build.1 = (bf16[4,768,768]{2,1,0:T(8,128)(2,1)S(1)}, bf16[4,768,768]{2,1,0:T(8,128)(2,1)S(1)}, bf16[4,768,768]{2,1,0:T(8,128)(2,1)S(1)}, bf16[4,768,768]{2,1,0:...) custom-call(s32[8]{0:T(128)S(1)} %stack.50.order_ref, ...), custom_call_target="tpu_custom_call" | custom-call | flops 8000000000 | bytes 38000000 | tf_op jit(solution)/shard_map/build/pallas_call | solution.py:549
  31.3 0.0 collective-permute-done.3.x3_ref
  31.3 2.6 %collective-permute-done.2.x2_ref = bf16[144,768]{1,0:T(8,128)(2,1)S(1)} collective-permute-done((bf16[144,768]{1,0:T(8,128)(2,1)}, bf16[144,768]{1,0:T(8,128)(2,1)S(1)}, u32[]{:S(2)}, u32[]{:S(2)}) %collective-permute-start.2) | collective-permute-done | bytes 221216 | tf_op jit(solution)/shard_map/ppermute | solution.py:536
  33.9 0.7 copy-done.3
  34.6 0.9 %copy-done.4 = bf16[144,768]{1,0:T(8,128)(2,1)S(1)} copy-done((bf16[144,768]{1,0:T(8,128)(2,1)S(1)}, bf16[144,768]{1,0:T(8,128)(2,1)}, u32[]{:S(2)}) %copy-start.4) | copy-done | bytes 221208
  35.5 26.2 %chain.1.own = f32[4,144,768]{2,1,0:T(8,128)S(1)} custom-call(s32[8]{0:T(128)S(1)} %stack.50.order_ref, bf16[144,768]{1,0:T(8,128)(2,1)S(1)} %copy-done.1, bf16[144,768]{1,0:T(8,128)(2,1)S(1)} %copy-done.4, bf16[144,768]{1,0:T(8,128)(2,1)S(1)} %collective-permute-done.2.x2_ref, bf16[144,768]{1,0:T(8,128)(2,1)S(1)} %collective-permute-done.3.x3_ref, ...), custom_call_target="tpu_custom_call" | custom-call | flops 35000000512 | bytes 38000000 | tf_op jit(solution)/shard_map/chain/pallas_call | solution.py:571
  61.8 1.5 %dots.1 = (f32[4,128,768]{2,1,0:T(8,128)S(1)}, f32[32,8,128]{2,1,0:T(8,128)S(1)}, f32[32,128]{1,0:T(8,128)S(1)}) custom-call(s32[8]{0:T(128)S(1)} %stack.50.order_ref, f32[4,144,768]{2,1,0:T(8,128)S(1)} %chain.1.own, bf16[144,768]{1,0:T(8,128)(2,1)S(1)} %copy-done.1, f32[8,8,128]{2,1,0:T(8,128)S(1)} %all-to-all-done.shared_ref, f32[8,768]{1,0:T(8,128)S(1)} %copy-done.2), custom_call_target="tpu_custom_call" | custom-call | tf_op jit(solution)/shard_map/dots/pallas_call | solution.py:590
  63.3 12.8 %all_to_all.10.gram_ref = f32[32,8,128]{2,1,0:T(8,128)S(1)} all-to-all(f32[32,8,128]{2,1,0:T(8,128)S(1)} %get-tuple-element.36), channel_id=1, replica_groups=mesh['sub'=8,'grp'=4] {'sub','grp'}, dimensions={0} | all-to-all | bytes 262144 | tf_op jit(solution)/shard_map/all_to_all | solution.py:604
  76.1 2.3 %finish.1 = (f32[750,1,128]{2,1,0:T(1,128)}, f32[750,1,128]{2,1,0:T(1,128)}) custom-call(s32[8]{0:T(128)S(1)} %stack.50.order_ref, f32[32,8,128]{2,1,0:T(8,128)S(1)} %all_to_all.10.gram_ref, f32[32,128]{1,0:T(8,128)S(1)} %get-tuple-element.37.inverse, f32[4,128,768]{2,1,0:T(8,128)S(1)} %get-tuple-element.38.fields_ref, f32[4,144,768]{2,1,0:T(8,128)S(1)} %chain.1.own, ...), custom_call_target="tpu_custom_call" | custom-call | tf_op jit(solution)/shard_map/finish/pallas_call | solution.py:605
  (15 shorter events, 0.0 us)
Async XLA Ops:
  2.8 13.6 %collective-permute-start.5 = (f32[8,768]{1,0:T(8,128)}, f32[8,768]{1,0:T(8,128)S(1)}, u32[]{:S(2)}, u32[]{:S(2)}) collective-permute-start(f32[8,768]{1,0:T(8,128)} %get-tuple-element.23), channel_id=1, source_target_pairs={{0,3},{1,2},{2,1},{3,0},{4,7},{5,6},{6,5},{7,4},{8,11},{9,10},{10,... | collective-permute-start | bytes 73736 | tf_op jit(solution)/shard_map/ppermute | solution.py:536
  8.0 8.5 %collective-permute-start.4 = (f32[8,768]{1,0:T(8,128)}, f32[8,768]{1,0:T(8,128)S(1)}, u32[]{:S(2)}, u32[]{:S(2)}) collective-permute-start(f32[8,768]{1,0:T(8,128)} %get-tuple-element.23), channel_id=1, source_target_pairs={{0,2},{1,3},{2,0},{3,1},{4,6},{5,7},{6,4},{7,5},{8,10},{9,11},{10,... | collective-permute-start | bytes 73736 | tf_op jit(solution)/shard_map/ppermute | solution.py:536
  8.0 4.0 %collective-permute-start = (f32[8,768]{1,0:T(8,128)}, f32[8,768]{1,0:T(8,128)S(1)}, u32[]{:S(2)}, u32[]{:S(2)}) collective-permute-start(f32[8,768]{1,0:T(8,128)} %get-tuple-element.23), channel_id=1, source_target_pairs={{0,1},{1,0},{2,3},{3,2},{4,5},{5,4},{6,7},{7,6},{8,9},{9,8},{10,11... | collective-permute-start | bytes 73736 | tf_op jit(solution)/shard_map/ppermute | solution.py:536
  12.0 19.3 %collective-permute-start.3 = (bf16[144,768]{1,0:T(8,128)(2,1)}, bf16[144,768]{1,0:T(8,128)(2,1)S(1)}, u32[]{:S(2)}, u32[]{:S(2)}) collective-permute-start(bf16[144,768]{1,0:T(8,128)(2,1)} %get-tuple-element.24.x0_ref), channel_id=1, source_target_pairs={{0,3},{1,2},{2,1},{3,0},{4,7},{5,6},{6,5},{7,4},{8,11},{9,10},{10,... | collective-permute-start | bytes 663560 | tf_op jit(solution)/shard_map/ppermute | solution.py:536
  15.8 18.1 %collective-permute-start.2 = (bf16[144,768]{1,0:T(8,128)(2,1)}, bf16[144,768]{1,0:T(8,128)(2,1)S(1)}, u32[]{:S(2)}, u32[]{:S(2)}) collective-permute-start(bf16[144,768]{1,0:T(8,128)(2,1)} %get-tuple-element.24.x0_ref), channel_id=1, source_target_pairs={{0,2},{1,3},{2,0},{3,1},{4,6},{5,7},{6,4},{7,5},{8,10},{9,11},{10,... | collective-permute-start | bytes 663560 | tf_op jit(solution)/shard_map/ppermute | solution.py:536
  15.8 18.1 %collective-permute-start.1 = (bf16[144,768]{1,0:T(8,128)(2,1)}, bf16[144,768]{1,0:T(8,128)(2,1)S(1)}, u32[]{:S(2)}, u32[]{:S(2)}) collective-permute-start(bf16[144,768]{1,0:T(8,128)(2,1)} %get-tuple-element.24.x0_ref), channel_id=1, source_target_pairs={{0,1},{1,0},{2,3},{3,2},{4,5},{5,4},{6,7},{7,6},{8,9},{9,8},{10,11... | collective-permute-start | bytes 663560 | tf_op jit(solution)/shard_map/ppermute | solution.py:536
  17.8 43.9 %all-to-all-start = ((f32[8,8,128]{2,1,0:T(8,128)}), f32[8,8,128]{2,1,0:T(8,128)S(1)}, u32[]{:S(2)}, u32[]{:S(2)}) async-start(f32[8,8,128]{2,1,0:T(8,128)} %broadcast_in_dim.11), calls=%async_computation | async-start | bytes 65536 | tf_op jit(solution)/shard_map/all_to_all | solution.py:544
  21.7 12.9 %copy-start.1 = (bf16[144,768]{1,0:T(8,128)(2,1)S(1)}, bf16[144,768]{1,0:T(8,128)(2,1)}, u32[]{:S(2)}) copy-start(bf16[144,768]{1,0:T(8,128)(2,1)} %get-tuple-element.24.x0_ref) | copy-start | bytes 663556
  33.9 0.7 copy-start.3
  34.6 0.9 %copy-start.4 = (bf16[144,768]{1,0:T(8,128)(2,1)S(1)}, bf16[144,768]{1,0:T(8,128)(2,1)}, u32[]{:S(2)}) copy-start(bf16[144,768]{1,0:T(8,128)(2,1)} %copy-done.3) | copy-start | bytes 663556
  35.5 26.2 %copy-start.2 = (f32[8,768]{1,0:T(8,128)S(1)}, f32[8,768]{1,0:T(8,128)}, u32[]{:S(2)}) copy-start(f32[8,768]{1,0:T(8,128)} %get-tuple-element.35.wide_ref) | copy-start | bytes 73732
  35.5 40.6 %copy-start = (f32[768,128]{1,0:T(8,128)S(1)}, f32[768,128]{1,0:T(8,128)}, u32[]{:S(2)}) copy-start(f32[768,128]{1,0:T(8,128)} %get-tuple-element.39.padded) | copy-start | bytes 1179652

commit v3 on v2

--- a/solution.py
+++ b/solution.py
@@ -33,16 +33,23 @@
     owner_hbm,
     home_hbm,
     moduli_hbm,
+    stiffness_hbm,
+    solve_hbm,
     packed_ref,
     table_ref,
+    shared_ref,
     padded,
     wide_ref,
+    order_ref,
+    matrices_ref,
     basis_ref,
     inverse_ref,
     send_ref,
     owner_ref,
     home_ref,
     moduli_ref,
+    stiffness_ref,
+    solve_ref,
     square,
     arrived,
 ):
@@ -52,6 +59,7 @@
     half = table_ref.shape[1]
     members, capacity = send_ref.shape
     local = home_ref.shape[1]
+    slab, member = lax.axis_index("sub"), lax.axis_index("grp")
     copies = [
         pltpu.make_async_copy(source, target, arrived.at[at])
         for at, (source, target) in enumerate(
@@ -63,6 +71,8 @@
                 (owner_hbm, owner_ref),
                 (home_hbm, home_ref),
                 (moduli_hbm, moduli_ref),
+                (stiffness_hbm, stiffness_ref),
+                (solve_hbm, solve_ref),
             )
         )
     ]
@@ -71,29 +81,45 @@
     padded[owned:, :] = jnp.zeros((wide - owned, loads), f32)
     wide_ref[...] = jnp.zeros_like(wide_ref)
     table_ref[...] = jnp.full(table_ref.shape, -1.0, f32)
+    matrices_ref[...] = jnp.zeros_like(matrices_ref)
     for copy in copies:
         copy.wait()
+    size = stiffness_ref.shape[0]
+    matrices_ref[0, :size, :size] = stiffness_ref[...]
+    matrices_ref[1, :size, :size] = solve_ref[...]
+
+    apart = lax.broadcasted_iota(jnp.int32, (members, LANES), 0) ^ member
+    unused = (send_ref[:, :LANES] >= local) & (apart > 0)
+    unused = unused & (lax.broadcasted_iota(jnp.int32, (members, LANES), 1) == 0)
+    opposite = jnp.sum(jnp.where(unused, apart.astype(f32), 0.0)).astype(jnp.int32)
+    opposite = jnp.minimum(jnp.maximum(opposite, 1), PLACES - 1)
+    near = jnp.where(opposite == 1, 2, 1)
+    order = (near, opposite, 6 - near - opposite, member, slab, slab, slab, slab)
+    for at, value in enumerate(order):
+        order_ref[at] = value
+
     wide_ref[0:1, :owned] = basis_ref[...]
     basis = wide_ref[0:1, :]
     term = jnp.zeros((loads, 1), f32)
     for start in range(0, wide, LANES):
         turned = padded[start : start + LANES, :].T
-        packed_ref[:loads, start : start + LANES] = turned.astype(bf16)
+        packed_ref[:, start : start + LANES] = turned.astype(bf16)
         term = term + jnp.sum(
             turned * basis[:, start : start + LANES], axis=1, keepdims=True
         )
-    row_ids = lax.broadcasted_iota(jnp.int32, (RIDERS, wide), 0)
-    packed_ref[loads:, :] = jnp.where(row_ids == 0, basis, 0.0).astype(bf16)
 
     table_ref[0:1, :] = home_ref[:, :half].astype(f32)
     table_ref[1:2, : local - half] = home_ref[:, half:].astype(f32)
     table_ref[2 : 2 + members, :capacity] = send_ref[...].astype(f32)
     table_ref[2 : 2 + members, half // 2 : half // 2 + capacity] = owner_ref[...].astype(f32)
-    table_ref[6:7, : moduli_ref.shape[1]] = moduli_ref[...]
+    table_ref[6:7, :] = basis
     square[...] = jnp.broadcast_to(term, square.shape)
-    table_ref[7:8, :] = jnp.zeros((1, half), f32)
-    table_ref[7:8, :LANES] = square[...].T[0:1, :]
-    table_ref[7:8, LANES : LANES + inverse_ref.shape[1]] = inverse_ref[...]
+    own_term = square[...].T[0:1, :]
+    square[0:1, :] = own_term
+    square[1:2, :] = jnp.zeros((1, LANES), f32)
+    square[1:2, : inverse_ref.shape[1]] = inverse_ref[...]
+    shared_ref[...] = jnp.broadcast_to(square[0:2, :][None], shared_ref.shape)
+    table_ref[7:8, : moduli_ref.shape[1]] = moduli_ref[...]
 
 
 def build_kernel(
@@ -101,7 +127,10 @@
     owned_count,
     local_count,
     order_ref,
-    tables,
+    t0_ref,
+    t1_ref,
+    t2_ref,
+    t3_ref,
     pick0,
     pick1,
     pick2,
@@ -111,6 +140,8 @@
     put2,
     put3,
     factors,
+    riders,
+    tables,
     slots,
     homes,
     sources,
@@ -124,15 +155,21 @@
     distance = place_distances(order_ref)
     member = order_ref[3]
     elements = 4
+    for at, table_ref in enumerate((t0_ref, t1_ref, t2_ref, t3_ref)):
+        tables[at] = table_ref[...]
     sources[...] = jnp.full(sources.shape, -1.0, f32)
     slots[...] = jnp.full(slots.shape, -1.0, f32)
     homes[...] = jnp.zeros_like(homes)
     lane_block = lax.broadcasted_iota(jnp.int32, (8, block), 1)
+    rider_ids = lax.broadcasted_iota(jnp.int32, (RIDERS, owned), 0)
     for place in range(PLACES):
+        riders[place] = jnp.where(
+            rider_ids == place, tables[distance[place], 6:7, :], 0.0
+        ).astype(bf16)
         homes[place : place + 1, :half] = tables[distance[place], 0:1, :]
         homes[place : place + 1, half:] = tables[distance[place], 1:2, :]
         for e in range(elements):
-            modulus = jnp.broadcast_to(tables[distance[place], 6:7, e : e + 1], (1, block))
+            modulus = jnp.broadcast_to(tables[distance[place], 7:8, e : e + 1], (1, block))
             factors[0, place, e : e + 1, :] = modulus
             factors[1, place, e : e + 1, :] = 1.0 / modulus
 
@@ -169,9 +206,10 @@
     sources_t[...] = sources[...].T
 
     chunk = 256
-    lane_ids = lax.broadcasted_iota(jnp.int32, (chunk, owned), 1).astype(f32)
-    deep_ids = lax.broadcasted_iota(jnp.int32, (chunk, half), 0).astype(f32)
+    deep_ids = lax.broadcasted_iota(jnp.int32, (chunk, LANES), 0).astype(f32).astype(bf16)
+    lane_ids = lax.broadcasted_iota(jnp.int32, (chunk, chunk), 1).astype(f32).astype(bf16)
     column_ids = lax.broadcasted_iota(jnp.int32, (chunk, LANES), 1)
+    one, zero = jnp.ones((), bf16), jnp.zeros((), bf16)
 
     for kind, (pick, put) in enumerate(zip(picks, puts)):
 
@@ -179,18 +217,24 @@
             n = kind * PLACES + place
             source = sources[pl.ds(n, 1), :]
             for start in range(0, owned, chunk):
-                pick[place, start : start + chunk, :] = jnp.where(
-                    deep_ids == source - float(start), 1.0, 0.0
-                ).astype(bf16)
+                moved = (source - float(start)).astype(bf16)
+                for at in range(0, half, LANES):
+                    wanted = jnp.broadcast_to(moved[:, at : at + LANES], (chunk, LANES))
+                    pick[place, start : start + chunk, at : at + LANES] = jnp.where(
+                        deep_ids == wanted, one, zero
+                    )
             for start in range(0, half, chunk):
                 column = jnp.sum(
                     jnp.where(column_ids == n, sources_t[start : start + chunk, :], 0.0),
                     axis=1,
                     keepdims=True,
                 )
-                put[place, start : start + chunk, :] = jnp.where(
-                    lane_ids == column, 1.0, 0.0
-                ).astype(bf16)
+                for at in range(0, owned, chunk):
+                    wanted = jnp.broadcast_to(column - float(at), (chunk, LANES)).astype(bf16)
+                    wanted = jnp.concatenate([wanted] * (chunk // LANES), axis=1)
+                    put[place, start : start + chunk, at : at + chunk] = jnp.where(
+                        lane_ids == wanted, one, zero
+                    )
             return carry
 
         lax.fori_loop(0, PLACES, build, 0)
@@ -211,12 +255,12 @@
     put2,
     put3,
     factors,
+    riders,
     matrices_ref,
     own,
     values,
     terms,
     copies,
-    riders,
 ):
     owned, half = pick0.shape[1], pick0.shape[2]
     block = matrices_ref.shape[1]
@@ -225,13 +269,10 @@
     f32, bf16 = jnp.float32, jnp.bfloat16
     distance = place_distances(order_ref)
     for at, x_ref in enumerate((x0_ref, x1_ref, x2_ref, x3_ref)):
-        values[1, at] = x_ref[...]
-    row_ids = lax.broadcasted_iota(jnp.int32, (RIDERS, owned), 0)
+        values[1, at, :loads, :] = x_ref[...]
     for place in range(PLACES):
-        values[0, place] = values[1, distance[place]]
-        riders[place] = jnp.where(
-            row_ids == place, values[0, place, loads : loads + 1, :].astype(f32), 0.0
-        ).astype(bf16)
+        values[0, place, :loads, :] = values[1, distance[place], :loads, :]
+        values[0, place, loads:, :] = jnp.zeros((RIDERS, owned), bf16)
 
     def multiply(left, right):
         return jnp.dot(left, right, preferred_element_type=f32)
@@ -305,22 +346,20 @@
     shared_ref,
     wide_ref,
     fields_ref,
+    images_ref,
     gram_ref,
     inverse,
     coarse_ref,
     square,
 ):
     f32 = jnp.float32
-    devices = inverse.shape[0]
     loads = fields_ref.shape[1]
     distance = place_distances(order_ref)
+    devices = inverse.shape[0]
     member = order_ref[3]
     first = order_ref[4] * PLACES
-    for at in range(devices // PLACES):
-        for apart in range(PLACES):
-            row = pl.ds(at * PLACES + (member ^ apart), 1)
-            coarse_ref[row, :] = shared_ref[at, apart : apart + 1, :]
-            inverse[row, :] = shared_ref[at, PLACES + apart : PLACES + apart + 1, :]
+    coarse_ref[...] = shared_ref[:, 0, :]
+    inverse[...] = shared_ref[:, 1, :]
     square[...] = jnp.zeros_like(square)
     for place in range(PLACES):
         square[place : place + 1, :] = inverse[pl.ds(first + (member ^ distance[place]), 1), :]
@@ -348,7 +387,8 @@
     fields_ref[1] = next_field
     fields_ref[2] = start_image
     fields_ref[3] = next_image
-    residual = x0_ref[:loads, :].astype(f32)
+    images_ref[...] = own[1, loads : loads + 8, :]
+    residual = x0_ref[...].astype(f32)
     lanes = lax.broadcasted_iota(jnp.int32, square.shape, 1)
     collected = jnp.zeros(square.shape, f32)
     for at, product in enumerate(
@@ -380,7 +420,7 @@
     gram_ref,
     inverse,
     fields_ref,
-    own,
+    images_ref,
     wide_ref,
     padded,
     solution_hbm,
@@ -393,7 +433,7 @@
 ):
     f32 = jnp.float32
     count = inverse.shape[0]
-    owned, _, loads = solution_hbm.shape
+    owned = solution_hbm.shape[0]
     first = order_ref[4] * PLACES
     member = order_ref[3]
     distance = place_distances(order_ref)
@@ -436,8 +476,8 @@
         )
         change = back * fields_ref[3, :, part] - whole * fields_ref[2, :, part]
         for place in range(PLACES):
-            row = loads + place
-            change = change + columns[:, 2 + place : 3 + place] * own[1, row : row + 1, part]
+            image = images_ref[place : place + 1, part]
+            change = change + columns[:, 2 + place : 3 + place] * image
         iterates[start : start + LANES, :] = iterate.T
         residuals[start : start + LANES, :] = padded[start : start + LANES, :] + change.T
         rows = slice(start, start + size)
@@ -475,24 +515,39 @@
     half = 2 * block
     devices = mesh_shape["sub"] * mesh_shape["grp"]
     rows = loads + RIDERS
-    slab = lax.axis_index("sub")
-    member = lax.axis_index("grp")
+    fits = half == owned_wide and loads == LANES and moduli.shape[2] == 4
+    fits = fits and send_index.shape[3] <= half // 2 and devices <= LANES
+    if not fits:
+        return exchange_body(
+            forces,
+            stiffness,
+            local_solve,
+            moduli,
+            coarse_basis,
+            coarse_inverse,
+            send_index,
+            owner_slot,
+            home_slot,
+        )
     smem = pl.BlockSpec(memory_space=pltpu.SMEM)
     vmem = pl.BlockSpec(memory_space=pltpu.VMEM)
 
     anywhere = pl.BlockSpec(memory_space=pltpu.HBM)
     slabs = mesh_shape["sub"]
 
-    packed, table, padded, wide = pl.pallas_call(
+    packed, table, shared, padded, wide, order, matrices = pl.pallas_call(
         pack_kernel,
         out_shape=(
-            jax.ShapeDtypeStruct((rows, owned_wide), bf16),
+            jax.ShapeDtypeStruct((loads, owned_wide), bf16),
             jax.ShapeDtypeStruct((8, half), f32),
+            jax.ShapeDtypeStruct((devices, 2, LANES), f32),
             jax.ShapeDtypeStruct((owned_wide, loads), f32),
             jax.ShapeDtypeStruct((8, owned_wide), f32),
+            jax.ShapeDtypeStruct((8,), i32),
+            jax.ShapeDtypeStruct((2, block, block), bf16),
         ),
-        in_specs=[anywhere] * 7,
-        out_specs=(vmem,) * 4,
+        in_specs=[anywhere] * 9,
+        out_specs=(vmem,) * 5 + (smem, vmem),
         scratch_shapes=[
             pltpu.VMEM((1, owned_count), f32),
             pltpu.VMEM((1, devices), f32),
@@ -500,8 +555,10 @@
             pltpu.VMEM(owner_slot.shape[2:], i32),
             pltpu.VMEM((1, local_count), i32),
             pltpu.VMEM((1, moduli.shape[2]), f32),
+            pltpu.VMEM((size, size), bf16),
+            pltpu.VMEM((size, size), bf16),
             pltpu.VMEM((LANES, LANES), f32),
-            pltpu.SemaphoreType.DMA((7,)),
+            pltpu.SemaphoreType.DMA((9,)),
         ],
         compiler_params=pltpu.CompilerParams(vmem_limit_bytes=62 * 2**20),
         name="pack",
@@ -513,91 +570,72 @@
         owner_slot[0, 0],
         home_slot[0],
         moduli[0],
+        stiffness,
+        local_solve,
     )
-
-    used = send_index[0, 0, :, 0] < local_count
-    distances = jnp.arange(PLACES, dtype=i32) ^ member
-    opposite = jnp.clip(jnp.sum(jnp.where(used, 0, distances)), 1, PLACES - 1)
-    near = jnp.where(opposite == 1, 2, 1)
-    order = jnp.stack(
-        [
-            near,
-            opposite,
-            6 - near - opposite,
-            member,
-            slab,
-            slab,
-            slab,
-            slab,
-        ]
-    ).astype(i32)
 
     def swapped(array, distance):
         return lax.ppermute(array, "grp", [(i, i ^ distance) for i in range(PLACES)])
 
     near_table = swapped(table, 1)
-    packed, near_table = lax.optimization_barrier((packed, near_table))
-    tables = jnp.stack([table, near_table, swapped(table, 2), swapped(table, 3)])
-    fields = [packed] + [swapped(packed, d) for d in range(1, PLACES)]
-    shared = jnp.concatenate([tables[:, 7, :LANES], tables[:, 7, LANES : 2 * LANES]], axis=0)
-    shared = jnp.broadcast_to(shared[None], (slabs, 8, LANES))
-    shared = lax.all_to_all(shared, "sub", split_axis=0, concat_axis=0, tiled=True)
-
-    widen = ((0, block - size), (0, block - size))
-    matrices = jnp.stack([jnp.pad(stiffness, widen), jnp.pad(local_solve, widen)])
-
-    *choices, factors = pl.pallas_call(
+    late, near_table = lax.optimization_barrier((packed, near_table))
+    tables = [table, near_table, swapped(table, 2), swapped(table, 3)]
+    fields = [packed, swapped(late, 1), swapped(packed, 2), swapped(packed, 3)]
+    shared = lax.all_to_all(shared, axes, split_axis=0, concat_axis=0, tiled=True)
+
+    *choices, factors, riders = pl.pallas_call(
         functools.partial(build_kernel, size, owned_count, local_count),
         out_shape=(
             *[jax.ShapeDtypeStruct((PLACES, owned_wide, half), bf16)] * 4,
             *[jax.ShapeDtypeStruct((PLACES, half, owned_wide), bf16)] * 4,
             jax.ShapeDtypeStruct((2, PLACES, 4, block), f32),
+            jax.ShapeDtypeStruct((PLACES, RIDERS, owned_wide), bf16),
         ),
-        in_specs=[smem, vmem],
-        out_specs=(vmem,) * 9,
+        in_specs=[smem] + [vmem] * 4,
+        out_specs=(vmem,) * 10,
         scratch_shapes=[
+            pltpu.VMEM((PLACES, 8, half), f32),
             pltpu.VMEM((LANES, half // 2), f32),
             pltpu.VMEM((8, 2 * half), f32),
             pltpu.VMEM((LANES, half), f32),
             pltpu.VMEM((half, LANES), f32),
         ],
-        compiler_params=pltpu.CompilerParams(vmem_limit_bytes=8 * 2**20),
+        compiler_params=pltpu.CompilerParams(vmem_limit_bytes=4 * 2**20),
         cost_estimate=pl.CostEstimate(
             flops=8 * 10**9, bytes_accessed=38 * 10**6, transcendentals=0
         ),
         name="build",
-    )(order, tables)
+    )(order, *tables)
 
     own = pl.pallas_call(
         chain_kernel,
         out_shape=jax.ShapeDtypeStruct((4, rows, owned_wide), f32),
-        in_specs=[smem] + [vmem] * 14,
+        in_specs=[smem] + [vmem] * 15,
         out_specs=vmem,
         scratch_shapes=[
             pltpu.VMEM((2, PLACES, rows, owned_wide), bf16),
             pltpu.VMEM((PLACES, 4, rows, block), bf16),
             pltpu.VMEM((PLACES, 4, rows, block), bf16),
-            pltpu.VMEM((PLACES, RIDERS, owned_wide), bf16),
         ],
-        compiler_params=pltpu.CompilerParams(vmem_limit_bytes=14 * 2**20),
+        compiler_params=pltpu.CompilerParams(vmem_limit_bytes=9 * 2**20),
         cost_estimate=pl.CostEstimate(
             flops=35 * 10**9, bytes_accessed=38 * 10**6, transcendentals=0
         ),
         name="chain",
-    )(order, *fields, *choices, factors, matrices)
-
-
-    results, gram, inverse = pl.pallas_call(
+    )(order, *fields, *choices, factors, riders, matrices)
+
+    results, images, gram, inverse = pl.pallas_call(
         dots_kernel,
         out_shape=(
             jax.ShapeDtypeStruct((4, loads, owned_wide), f32),
+            jax.ShapeDtypeStruct((8, owned_wide), f32),
             jax.ShapeDtypeStruct((devices, 8, LANES), f32),
             jax.ShapeDtypeStruct((devices, LANES), f32),
         ),
         in_specs=[smem] + [vmem] * 4,
-        out_specs=(vmem,) * 3,
+        out_specs=(vmem,) * 4,
         scratch_shapes=[pltpu.VMEM((devices, LANES), f32), pltpu.VMEM((LANES, LANES), f32)],
-        compiler_params=pltpu.CompilerParams(vmem_limit_bytes=8 * 2**20),
+        compiler_params=pltpu.CompilerParams(vmem_limit_bytes=4 * 2**20),
         name="dots",
     )(order, own, packed, shared, wide)
 
@@ -614,9 +652,9 @@
             pltpu.VMEM((owned_wide, loads), f32),
             pltpu.SemaphoreType.DMA((2, owned_wide // LANES)),
         ],
-        compiler_params=pltpu.CompilerParams(vmem_limit_bytes=8 * 2**20),
+        compiler_params=pltpu.CompilerParams(vmem_limit_bytes=4 * 2**20),
         name="finish",
-    )(order, gathered, inverse, results, own, wide, padded)
+    )(order, gathered, inverse, results, images, wide, padded)
     return (iterate.reshape(forces.shape), residual.reshape(forces.shape))
 
 

time: 78.9 us -> 72 us (0.913)
  Pallas kernels: 41.7 us -> 39.1 us
  other arithmetic: 2.29 us -> 0 us
  local copies, waits for them, and re-layouts: 3.45 us -> 1.36 us
  blocking collectives: 12.8 us -> 11.3 us
  starting transfers between devices: 14.1 us -> 15.6 us
  waiting for transfers between devices: 2.65 us -> 3.46 us
    all_to_all x1, blocking collectives: 12.8 us -> 11.3 us  [slab_body(): lax.all_to_all(gram, axes, split_axis=0, concat_axis=0, tiled=True)]
    pallas_call x1, Pallas kernels: 9.57 us -> 8.02 us  [slab_body(): pl.pallas_call(functools.partial(build_kernel, size, owned_count, local_c...]
    pallas_call x1, Pallas kernels: 26.2 us -> 24.8 us  [slab_body(): pl.pallas_call(chain_kernel, out_shape=jax.ShapeDtypeStruct((4, rows, own...]
    another operation x2 -> x0, local copies, waits for them, and re-layouts: 1.2 us -> none  [the longest x1 1.11 us: slab_body(): jnp.stack([jnp.pad(stiffness, widen), jnp.pad(local_solve, widen)])]
    all_to_all x1, starting transfers between devices: 3.87 us -> 4.84 us  [slab_body(): lax.all_to_all(shared, axes, split_axis=0, concat_axis=0, tiled=True)]
    another operation x2 -> x0, other arithmetic: 0.82 us -> none  [the longest x1 0.75 us: slab_body(): jnp.stack([table, near_table, swapped(table, 2), swapped(table, 3)])]
    ppermute x6, waiting for transfers between devices: 2.65 us -> 3.46 us  [swapped(): lax.ppermute(array, 'grp', [(i, i ^ distance) for i in range(PLACES)])]
    lt x1 -> x0, other arithmetic: 0.8 us -> none  [slab_body(): used = send_index[0, 0, :, 0] < local_count]
  transfers between devices with their start and end apart: 7 -> 7, of which waited for: 1 -> 1; matrix products, arithmetic and copies ran while one was open for 5% -> 0% of each run, Pallas kernels for 46% -> 46%
where the time goes in v3:
time: 72 us; the launch traced here: 71.7 us
  Pallas kernels  39.1 us (54%)
  starting transfers between devices  15.6 us (22%)
  blocking collectives  11.3 us (16%)
  waiting for transfers between devices  3.46 us (5%)
  local copies, waits for them, and re-layouts  1.36 us (2%)
  between operations  0.93 us (1%)
    pallas_call x1, Pallas kernels, slab_body(): pl.pallas_call(chain_kernel, out_shape=jax.ShapeDtypeStruct((4, rows, own...  24.8 us
    all_to_all x1, blocking collectives, slab_body(): lax.all_to_all(gram, axes, split_axis=0, concat_axis=0, tiled=True)  11.3 us
    ppermute x6, starting transfers between devices, swapped(): lax.ppermute(array, 'grp', [(i, i ^ distance) for i in range(PLACES)])  10.8 us
    pallas_call x1, Pallas kernels, slab_body(): pl.pallas_call(functools.partial(build_kernel, size, owned_count, local_c...  8.02 us
    all_to_all x1, starting transfers between devices, slab_body(): lax.all_to_all(shared, axes, split_axis=0, concat_axis=0, tiled=True)  4.84 us
    ppermute x6, waiting for transfers between devices, swapped(): lax.ppermute(array, 'grp', [(i, i ^ distance) for i in range(PLACES)])  3.46 us
    pallas_call x1, Pallas kernels, slab_body(): pl.pallas_call(pack_kernel, out_shape=(jax.ShapeDtypeStruct((loads, owned...  2.54 us
    pallas_call x1, Pallas kernels, slab_body(): pl.pallas_call(finish_kernel, out_shape=(jax.ShapeDtypeStruct((owned_coun...  2.23 us
  transfers between devices with their start and end apart: 7, of which 1 were waited for; matrix products, arithmetic and copies ran while one was open for 0% of the time, Pallas kernels for 46%

profile of v3, /device:TPU:0, one launch (start us, length us, event | category | flops | bytes accessed | tf_op | source)
XLA Modules:
  0.0 71.7 jit_solution(8197918886220373470)
XLA Ops:
  0.6 2.5 %pack.1 = (bf16[128,768]{1,0:T(8,128)(2,1)}, f32[8,768]{1,0:T(8,128)}, f32[32,2,128]{2,1,0:T(2,128)}, f32[768,128]{1,0:T(8,128)}, f32[8,768]{1,0:T(8,128)}, /*index=5*/s32[8]{0:T(128)}, bf16[2,384,384]{2,1,0:T(8,128)(2,1)}) custom-call(f32[750,1,128]{2,1,0:T(1,128)} %bitcast.12, f32[1,750]{1,0:T(1,128)} %bitcast.16, f32[1,32]{1,0:T(1,128)} %inverse_hbm.1, ...), custom_call_target="tpu_custom_call" | custom-call | tf_op jit(solution)/shard_map/pack/pallas_call | solution.py:538
  3.2 3.1 %collective-permute-start = (f32[8,768]{1,0:T(8,128)}, f32[8,768]{1,0:T(8,128)S(1)}, u32[]{:S(2)}, u32[]{:S(2)}) collective-permute-start(f32[8,768]{1,0:T(8,128)} %get-tuple-element.29.t0_ref), channel_id=1, source_target_pairs={{0,1},{1,0},{2,3},{3,2},{4,5},{5,4},{6,7},{7,6},{8,9},{9,8},{10,11... | collective-permute-start | bytes 73736 | tf_op jit(solution)/shard_map/ppermute | solution.py:578
  6.3 2.5 %collective-permute-start.5 = (f32[8,768]{1,0:T(8,128)}, f32[8,768]{1,0:T(8,128)S(1)}, u32[]{:S(2)}, u32[]{:S(2)}) collective-permute-start(f32[8,768]{1,0:T(8,128)} %get-tuple-element.29.t0_ref), channel_id=1, source_target_pairs={{0,3},{1,2},{2,1},{3,0},{4,7},{5,6},{6,5},{7,4},{8,11},{9,10},{10,... | collective-permute-start | bytes 73736 | tf_op jit(solution)/shard_map/ppermute | solution.py:578
  8.7 0.1 collective-permute-start.4
  8.9 2.9 %collective-permute-start.3 = (bf16[128,768]{1,0:T(8,128)(2,1)}, bf16[128,768]{1,0:T(8,128)(2,1)S(1)}, u32[]{:S(2)}, u32[]{:S(2)}) collective-permute-start(bf16[128,768]{1,0:T(8,128)(2,1)} %get-tuple-element.30.x0_ref), channel_id=1, source_target_pairs={{0,3},{1,2},{2,1},{3,0},{4,7},{5,6},{6,5},{7,4},{8,11},{9,10},{10,... | collective-permute-start | bytes 589832 | tf_op jit(solution)/shard_map/ppermute | solution.py:578
  11.8 0.3 collective-permute-start.2
  12.1 4.8 %all-to-all-start = ((f32[32,2,128]{2,1,0:T(2,128)}), f32[32,2,128]{2,1,0:T(2,128)S(1)}, u32[]{:S(2)}, u32[]{:S(2)}) async-start(f32[32,2,128]{2,1,0:T(2,128)} %get-tuple-element.43), calls=%async_computation | async-start | bytes 65536 | tf_op jit(solution)/shard_map/all_to_all | solution.py:584
  17.0 0.0 collective-permute-done.t1_ref
  17.0 1.8 %collective-permute-start.1 = (bf16[128,768]{1,0:T(8,128)(2,1)}, bf16[128,768]{1,0:T(8,128)(2,1)S(1)}, u32[]{:S(2)}, u32[]{:S(2)}) collective-permute-start(bf16[128,768]{1,0:T(8,128)(2,1)} %get-tuple-element.30.x0_ref), channel_id=1, source_target_pairs={{0,1},{1,0},{2,3},{3,2},{4,5},{5,4},{6,7},{7,6},{8,9},{9,8},{10,11... | collective-permute-start | bytes 589832 | tf_op jit(solution)/shard_map/ppermute | solution.py:578
  18.8 0.0 collective-permute-done.5.t3_ref
  18.8 3.4 %collective-permute-done.4.t2_ref = f32[8,768]{1,0:T(8,128)S(1)} collective-permute-done((f32[8,768]{1,0:T(8,128)}, f32[8,768]{1,0:T(8,128)S(1)}, u32[]{:S(2)}, u32[]{:S(2)}) %collective-permute-start.4) | collective-permute-done | bytes 24608 | tf_op jit(solution)/shard_map/ppermute | solution.py:578
  22.3 0.6 copy-done.3
  22.9 0.7 %copy-done.6 = f32[8,768]{1,0:T(8,128)S(1)} copy-done((f32[8,768]{1,0:T(8,128)S(1)}, f32[8,768]{1,0:T(8,128)}, u32[]{:S(2)}) %copy-start.6) | copy-done | bytes 24600
  23.6 8.0 %build.1 = (bf16[4,768,768]{2,1,0:T(8,128)(2,1)S(1)}, bf16[4,768,768]{2,1,0:T(8,128)(2,1)S(1)}, bf16[4,768,768]{2,1,0:T(8,128)(2,1)S(1)}, bf16[4,768,768]{2,1,0:...) custom-call(s32[8]{0:T(128)S(1)} %copy-done.3, ...), custom_call_target="tpu_custom_call" | custom-call | flops 8000000000 | bytes 38000000 | tf_op jit(solution)/shard_map/build/pallas_call | solution.py:586
  31.6 0.0 collective-permute-done.3.x3_ref
  31.6 0.0 collective-permute-done.2.x2_ref
  31.7 0.0 collective-permute-done.1.x1_ref
  31.7 0.0 copy-done.1
  31.7 0.0 copy-done.4
  31.7 24.8 %chain.1.own = f32[4,144,768]{2,1,0:T(8,128)S(1)} custom-call(s32[8]{0:T(128)S(1)} %copy-done.4, bf16[128,768]{1,0:T(8,128)(2,1)S(1)} %copy-done.1, bf16[128,768]{1,0:T(8,128)(2,1)S(1)} %collective-permute-done.1.x1_ref, bf16[128,768]{1,0:T(8,128)(2,1)S(1)} %collective-permute-done.2.x2_ref, bf16[128,768]{1,0:T(8,128)(2,1)S(1)} %collective-permute-done.3.x3_ref, ...), custom_call_target="tpu_custom_call" | custom-call | flops 35000000512 | bytes 38000000 | tf_op jit(solution)/shard_map/chain/pallas_call | solution.py:610
  56.5 0.0 all-to-all-done.shared_ref
  56.5 1.5 %dots.1 = (f32[4,128,768]{2,1,0:T(8,128)S(1)}, f32[8,768]{1,0:T(8,128)S(1)}, f32[32,8,128]{2,1,0:T(8,128)S(1)}, f32[32,128]{1,0:T(8,128)S(1)}) custom-call(s32[8]{0:T(128)S(1)} %copy-done.4, f32[4,144,768]{2,1,0:T(8,128)S(1)} %chain.1.own, bf16[128,768]{1,0:T(8,128)(2,1)S(1)} %copy-done.1, f32[32,2,128]{2,1,0:T(2,128)S(1)} %all-to-all-done.shared_ref, ...), custom_call_target="tpu_custom_call" | custom-call | tf_op jit(solution)/shard_map/dots/pallas_call | solution.py:627
  58.0 11.3 %all_to_all.10.gram_ref = f32[32,8,128]{2,1,0:T(8,128)S(1)} all-to-all(f32[32,8,128]{2,1,0:T(8,128)S(1)} %get-tuple-element.45), channel_id=1, replica_groups=mesh['sub'=8,'grp'=4] {'sub','grp'}, dimensions={0} | all-to-all | bytes 262144 | tf_op jit(solution)/shard_map/all_to_all | solution.py:642
  69.3 2.2 %finish.1 = (f32[750,1,128]{2,1,0:T(1,128)}, f32[750,1,128]{2,1,0:T(1,128)}) custom-call(s32[8]{0:T(128)S(1)} %copy-done.4, f32[32,8,128]{2,1,0:T(8,128)S(1)} %all_to_all.10.gram_ref, f32[32,128]{1,0:T(8,128)S(1)} %get-tuple-element.46.inverse, f32[4,128,768]{2,1,0:T(8,128)S(1)} %get-tuple-element.47.fields_ref, f32[8,768]{1,0:T(8,128)S(1)} %get-tuple-element.48.images_ref, ...), custom_call_target="tpu_custom_call" | custom-call | tf_op jit(solution)/shard_map/finish/pallas_call | solution.py:643
  (10 shorter events, 0.0 us)
Async XLA Ops:
  3.2 13.8 %collective-permute-start = (f32[8,768]{1,0:T(8,128)}, f32[8,768]{1,0:T(8,128)S(1)}, u32[]{:S(2)}, u32[]{:S(2)}) collective-permute-start(f32[8,768]{1,0:T(8,128)} %get-tuple-element.29.t0_ref), channel_id=1, source_target_pairs={{0,1},{1,0},{2,3},{3,2},{4,5},{5,4},{6,7},{7,6},{8,9},{9,8},{10,11... | collective-permute-start | bytes 73736 | tf_op jit(solution)/shard_map/ppermute | solution.py:578
  6.3 12.5 %collective-permute-start.5 = (f32[8,768]{1,0:T(8,128)}, f32[8,768]{1,0:T(8,128)S(1)}, u32[]{:S(2)}, u32[]{:S(2)}) collective-permute-start(f32[8,768]{1,0:T(8,128)} %get-tuple-element.29.t0_ref), channel_id=1, source_target_pairs={{0,3},{1,2},{2,1},{3,0},{4,7},{5,6},{6,5},{7,4},{8,11},{9,10},{10,... | collective-permute-start | bytes 73736 | tf_op jit(solution)/shard_map/ppermute | solution.py:578
  8.7 13.5 %collective-permute-start.4 = (f32[8,768]{1,0:T(8,128)}, f32[8,768]{1,0:T(8,128)S(1)}, u32[]{:S(2)}, u32[]{:S(2)}) collective-permute-start(f32[8,768]{1,0:T(8,128)} %get-tuple-element.29.t0_ref), channel_id=1, source_target_pairs={{0,2},{1,3},{2,0},{3,1},{4,6},{5,7},{6,4},{7,5},{8,10},{9,11},{10,... | collective-permute-start | bytes 73736 | tf_op jit(solution)/shard_map/ppermute | solution.py:578
  8.9 22.8 %collective-permute-start.3 = (bf16[128,768]{1,0:T(8,128)(2,1)}, bf16[128,768]{1,0:T(8,128)(2,1)S(1)}, u32[]{:S(2)}, u32[]{:S(2)}) collective-permute-start(bf16[128,768]{1,0:T(8,128)(2,1)} %get-tuple-element.30.x0_ref), channel_id=1, source_target_pairs={{0,3},{1,2},{2,1},{3,0},{4,7},{5,6},{6,5},{7,4},{8,11},{9,10},{10,... | collective-permute-start | bytes 589832 | tf_op jit(solution)/shard_map/ppermute | solution.py:578
  11.8 19.9 %collective-permute-start.2 = (bf16[128,768]{1,0:T(8,128)(2,1)}, bf16[128,768]{1,0:T(8,128)(2,1)S(1)}, u32[]{:S(2)}, u32[]{:S(2)}) collective-permute-start(bf16[128,768]{1,0:T(8,128)(2,1)} %get-tuple-element.30.x0_ref), channel_id=1, source_target_pairs={{0,2},{1,3},{2,0},{3,1},{4,6},{5,7},{6,4},{7,5},{8,10},{9,11},{10,... | collective-permute-start | bytes 589832 | tf_op jit(solution)/shard_map/ppermute | solution.py:578
  12.1 44.4 %all-to-all-start = ((f32[32,2,128]{2,1,0:T(2,128)}), f32[32,2,128]{2,1,0:T(2,128)S(1)}, u32[]{:S(2)}, u32[]{:S(2)}) async-start(f32[32,2,128]{2,1,0:T(2,128)} %get-tuple-element.43), calls=%async_computation | async-start | bytes 65536 | tf_op jit(solution)/shard_map/all_to_all | solution.py:584
  17.0 14.7 %collective-permute-start.1 = (bf16[128,768]{1,0:T(8,128)(2,1)}, bf16[128,768]{1,0:T(8,128)(2,1)S(1)}, u32[]{:S(2)}, u32[]{:S(2)}) collective-permute-start(bf16[128,768]{1,0:T(8,128)(2,1)} %get-tuple-element.30.x0_ref), channel_id=1, source_target_pairs={{0,1},{1,0},{2,3},{3,2},{4,5},{5,4},{6,7},{7,6},{8,9},{9,8},{10,11... | collective-permute-start | bytes 589832 | tf_op jit(solution)/shard_map/ppermute | solution.py:578
  22.3 0.6 copy-start.3
  22.9 0.7 %copy-start.6 = (f32[8,768]{1,0:T(8,128)S(1)}, f32[8,768]{1,0:T(8,128)}, u32[]{:S(2)}) copy-start(f32[8,768]{1,0:T(8,128)} %get-tuple-element.29.t0_ref) | copy-start | bytes 73732
  23.6 8.1 %copy-start.1 = (bf16[128,768]{1,0:T(8,128)(2,1)S(1)}, bf16[128,768]{1,0:T(8,128)(2,1)}, u32[]{:S(2)}) copy-start(bf16[128,768]{1,0:T(8,128)(2,1)} %get-tuple-element.30.x0_ref) | copy-start | bytes 589828
  23.6 8.1 %copy-start.4 = (s32[8]{0:T(128)S(1)}, s32[8]{0:T(128)}, u32[]{:S(2)}) copy-start(s32[8]{0:T(128)} %get-tuple-element.27.order_ref) | copy-start | bytes 100
  23.6 8.1 %copy-start.5 = (bf16[2,384,384]{2,1,0:T(8,128)(2,1)S(1)}, bf16[2,384,384]{2,1,0:T(8,128)(2,1)}, u32[]{:S(2)}) copy-start(bf16[2,384,384]{2,1,0:T(8,128)(2,1)} %get-tuple-element.42.matrices_ref) | copy-start | bytes 1769476
  31.7 24.8 %copy-start.2 = (f32[8,768]{1,0:T(8,128)S(1)}, f32[8,768]{1,0:T(8,128)}, u32[]{:S(2)}) copy-start(f32[8,768]{1,0:T(8,128)} %get-tuple-element.44.wide_ref) | copy-start | bytes 73732
  31.7 37.6 %copy-start = (f32[768,128]{1,0:T(8,128)S(1)}, f32[768,128]{1,0:T(8,128)}, u32[]{:S(2)}) copy-start(f32[768,128]{1,0:T(8,128)} %get-tuple-element.49.padded) | copy-start | bytes 1179652

commit v4 on v3

--- a/solution.py
+++ b/solution.py
@@ -33,23 +33,18 @@
     owner_hbm,
     home_hbm,
     moduli_hbm,
-    stiffness_hbm,
-    solve_hbm,
     packed_ref,
     table_ref,
     shared_ref,
     padded,
     wide_ref,
     order_ref,
-    matrices_ref,
     basis_ref,
     inverse_ref,
     send_ref,
     owner_ref,
     home_ref,
     moduli_ref,
-    stiffness_ref,
-    solve_ref,
     square,
     arrived,
 ):
@@ -71,8 +66,6 @@
                 (owner_hbm, owner_ref),
                 (home_hbm, home_ref),
                 (moduli_hbm, moduli_ref),
-                (stiffness_hbm, stiffness_ref),
-                (solve_hbm, solve_ref),
             )
         )
     ]
@@ -81,13 +74,8 @@
     padded[owned:, :] = jnp.zeros((wide - owned, loads), f32)
     wide_ref[...] = jnp.zeros_like(wide_ref)
     table_ref[...] = jnp.full(table_ref.shape, -1.0, f32)
-    matrices_ref[...] = jnp.zeros_like(matrices_ref)
     for copy in copies:
         copy.wait()
-    size = stiffness_ref.shape[0]
-    matrices_ref[0, :size, :size] = stiffness_ref[...]
-    matrices_ref[1, :size, :size] = solve_ref[...]
-
     apart = lax.broadcasted_iota(jnp.int32, (members, LANES), 0) ^ member
     unused = (send_ref[:, :LANES] >= local) & (apart > 0)
     unused = unused & (lax.broadcasted_iota(jnp.int32, (members, LANES), 1) == 0)
@@ -535,7 +523,7 @@
     anywhere = pl.BlockSpec(memory_space=pltpu.HBM)
     slabs = mesh_shape["sub"]
 
-    packed, table, shared, padded, wide, order, matrices = pl.pallas_call(
+    packed, table, shared, padded, wide, order = pl.pallas_call(
         pack_kernel,
         out_shape=(
             jax.ShapeDtypeStruct((loads, owned_wide), bf16),
@@ -544,10 +532,9 @@
             jax.ShapeDtypeStruct((owned_wide, loads), f32),
             jax.ShapeDtypeStruct((8, owned_wide), f32),
             jax.ShapeDtypeStruct((8,), i32),
-            jax.ShapeDtypeStruct((2, block, block), bf16),
         ),
-        in_specs=[anywhere] * 9,
-        out_specs=(vmem,) * 5 + (smem, vmem),
+        in_specs=[anywhere] * 7,
+        out_specs=(vmem,) * 5 + (smem,),
         scratch_shapes=[
             pltpu.VMEM((1, owned_count), f32),
             pltpu.VMEM((1, devices), f32),
@@ -555,10 +542,8 @@
             pltpu.VMEM(owner_slot.shape[2:], i32),
             pltpu.VMEM((1, local_count), i32),
             pltpu.VMEM((1, moduli.shape[2]), f32),
-            pltpu.VMEM((size, size), bf16),
-            pltpu.VMEM((size, size), bf16),
             pltpu.VMEM((LANES, LANES), f32),
-            pltpu.SemaphoreType.DMA((9,)),
+            pltpu.SemaphoreType.DMA((7,)),
         ],
         compiler_params=pltpu.CompilerParams(vmem_limit_bytes=62 * 2**20),
         name="pack",
@@ -570,8 +555,6 @@
         owner_slot[0, 0],
         home_slot[0],
         moduli[0],
-        stiffness,
-        local_solve,
     )
 
     def swapped(array, distance):
@@ -582,6 +565,9 @@
     tables = [table, near_table, swapped(table, 2), swapped(table, 3)]
     fields = [packed, swapped(late, 1), swapped(packed, 2), swapped(packed, 3)]
     shared = lax.all_to_all(shared, axes, split_axis=0, concat_axis=0, tiled=True)
+
+    widen = ((0, block - size), (0, block - size))
+    matrices = jnp.stack([jnp.pad(stiffness, widen), jnp.pad(local_solve, widen)])
 
     *choices, factors, riders = pl.pallas_call(
         functools.partial(build_kernel, size, owned_count, local_count),

time: 72 us -> 73.3 us (1.018)
  waiting for transfers between devices: 3.46 us -> 1.04 us
  blocking collectives: 11.3 us -> 13.4 us
  local copies, waits for them, and re-layouts: 1.36 us -> 2.44 us
  starting transfers between devices: 15.6 us -> 16.5 us
    ppermute x6, waiting for transfers between devices: 3.46 us -> 1.04 us  [swapped(): lax.ppermute(array, 'grp', [(i, i ^ distance) for i in range(PLACES)])]
    all_to_all x1, blocking collectives: 11.3 us -> 13.4 us  [slab_body(): lax.all_to_all(gram, axes, split_axis=0, concat_axis=0, tiled=True)]
    another operation x0 -> x1, local copies, waits for them, and re-layouts: none -> 1.12 us  [slab_body(): jnp.stack([jnp.pad(stiffness, widen), jnp.pad(local_solve, widen)])]
  transfers between devices with their start and end apart: 7 -> 7, of which waited for: 1 -> 1; matrix products, arithmetic and copies ran while one was open for 0% -> 2% of each run, Pallas kernels for 46% -> 45%
where the time goes in v4:
time: 73.3 us; the launch traced here: 73 us
  Pallas kernels  38.6 us (53%)
  starting transfers between devices  16.5 us (23%)
  blocking collectives  13.4 us (18%)
  local copies, waits for them, and re-layouts  2.44 us (3%)
  waiting for transfers between devices  1.04 us (1%)
  between operations  0.93 us (1%)
    pallas_call x1, Pallas kernels, slab_body(): pl.pallas_call(chain_kernel, out_shape=jax.ShapeDtypeStruct((4, rows, own...  24.8 us
    all_to_all x1, blocking collectives, slab_body(): lax.all_to_all(gram, axes, split_axis=0, concat_axis=0, tiled=True)  13.4 us
    ppermute x6, starting transfers between devices, swapped(): lax.ppermute(array, 'grp', [(i, i ^ distance) for i in range(PLACES)])  11.3 us
    pallas_call x1, Pallas kernels, slab_body(): pl.pallas_call(functools.partial(build_kernel, size, owned_count, local_c...  8.02 us
    all_to_all x1, starting transfers between devices, slab_body(): lax.all_to_all(shared, axes, split_axis=0, concat_axis=0, tiled=True)  5.17 us
    pallas_call x1, Pallas kernels, slab_body(): pl.pallas_call(finish_kernel, out_shape=(jax.ShapeDtypeStruct((owned_coun...  2.24 us
    pallas_call x1, Pallas kernels, slab_body(): pl.pallas_call(pack_kernel, out_shape=(jax.ShapeDtypeStruct((loads, owned...  2.05 us
    pallas_call x1, Pallas kernels, slab_body(): pl.pallas_call(dots_kernel, out_shape=(jax.ShapeDtypeStruct((4, loads, ow...  1.51 us
  transfers between devices with their start and end apart: 7, of which 1 were waited for; matrix products, arithmetic and copies ran while one was open for 2% of the time, Pallas kernels for 45%

profile of v4, /device:TPU:0, one launch (start us, length us, event | category | flops | bytes accessed | tf_op | source)
XLA Modules:
  0.0 73.0 jit_solution(1739325690580618790)
XLA Ops:
  0.6 2.0 %pack.1 = (bf16[128,768]{1,0:T(8,128)(2,1)}, f32[8,768]{1,0:T(8,128)}, f32[32,2,128]{2,1,0:T(2,128)}, f32[768,128]{1,0:T(8,128)}, f32[8,768]{1,0:T(8,128)}, /*index=5*/s32[8]{0:T(128)}) custom-call(f32[750,1,128]{2,1,0:T(1,128)} %bitcast.16, f32[1,750]{1,0:T(1,128)} %bitcast.20, f32[1,32]{1,0:T(1,128)} %inverse_hbm.1, s32[4,316]{1,0:T(4,128)} %bitcast.17, ...), custom_call_target="tpu_custom_call" | custom-call | tf_op jit(solution)/shard_map/pack/pallas_call | solution.py:526
  2.7 5.1 %collective-permute-start.5 = (f32[8,768]{1,0:T(8,128)}, f32[8,768]{1,0:T(8,128)S(1)}, u32[]{:S(2)}, u32[]{:S(2)}) collective-permute-start(f32[8,768]{1,0:T(8,128)} %get-tuple-element.28.t0_ref), channel_id=1, source_target_pairs={{0,3},{1,2},{2,1},{3,0},{4,7},{5,6},{6,5},{7,4},{8,11},{9,10},{10,... | collective-permute-start | bytes 73736 | tf_op jit(solution)/shard_map/ppermute | solution.py:561
  7.8 0.0 collective-permute-start.4
  7.8 0.6 collective-permute-start
  8.4 3.7 %collective-permute-start.3 = (bf16[128,768]{1,0:T(8,128)(2,1)}, bf16[128,768]{1,0:T(8,128)(2,1)S(1)}, u32[]{:S(2)}, u32[]{:S(2)}) collective-permute-start(bf16[128,768]{1,0:T(8,128)(2,1)} %get-tuple-element.29.x0_ref), channel_id=1, source_target_pairs={{0,3},{1,2},{2,1},{3,0},{4,7},{5,6},{6,5},{7,4},{8,11},{9,10},{10,... | collective-permute-start | bytes 589832 | tf_op jit(solution)/shard_map/ppermute | solution.py:561
  12.2 0.0 collective-permute-start.2
  12.2 5.2 %all-to-all-start = ((f32[32,2,128]{2,1,0:T(2,128)}), f32[32,2,128]{2,1,0:T(2,128)S(1)}, u32[]{:S(2)}, u32[]{:S(2)}) async-start(f32[32,2,128]{2,1,0:T(2,128)} %get-tuple-element.41), calls=%async_computation | async-start | bytes 65536 | tf_op jit(solution)/shard_map/all_to_all | solution.py:567
  17.4 1.1 %pad_bitcast_fusion = (bf16[1,384,384]{2,1,0:T(8,128)(2,1)S(1)}, bf16[1,384,384]{2,1,0:T(8,128)(2,1)S(1)}) fusion(bf16[375,375]{1,0:T(8,128)(2,1)} %param.11, bf16[375,375]{1,0:T(8,128)(2,1)} %param.10), kind=kLoop, calls=%fused_computation.1 | loop fusion | bytes 1152324 | tf_op jit(solution)/shard_map/stack | solution.py:570
  18.5 0.1 pad_maximum_fusion.matrices_ref
  18.6 0.0 collective-permute-done.t1_ref
  18.6 1.8 %collective-permute-start.1 = (bf16[128,768]{1,0:T(8,128)(2,1)}, bf16[128,768]{1,0:T(8,128)(2,1)S(1)}, u32[]{:S(2)}, u32[]{:S(2)}) collective-permute-start(bf16[128,768]{1,0:T(8,128)(2,1)} %get-tuple-element.29.x0_ref), channel_id=1, source_target_pairs={{0,1},{1,0},{2,3},{3,2},{4,5},{5,4},{6,7},{7,6},{8,9},{9,8},{10,11... | collective-permute-start | bytes 589832 | tf_op jit(solution)/shard_map/ppermute | solution.py:561
  20.4 0.0 collective-permute-done.5.t3_ref
  20.4 1.0 %collective-permute-done.4.t2_ref = f32[8,768]{1,0:T(8,128)S(1)} collective-permute-done((f32[8,768]{1,0:T(8,128)}, f32[8,768]{1,0:T(8,128)S(1)}, u32[]{:S(2)}, u32[]{:S(2)}) %collective-permute-start.4) | collective-permute-done | bytes 24608 | tf_op jit(solution)/shard_map/ppermute | solution.py:561
  21.4 0.6 copy-done.3
  22.0 0.7 %copy-done.5 = f32[8,768]{1,0:T(8,128)S(1)} copy-done((f32[8,768]{1,0:T(8,128)S(1)}, f32[8,768]{1,0:T(8,128)}, u32[]{:S(2)}) %copy-start.5) | copy-done | bytes 24600
  22.8 8.0 %build.1 = (bf16[4,768,768]{2,1,0:T(8,128)(2,1)S(1)}, bf16[4,768,768]{2,1,0:T(8,128)(2,1)S(1)}, bf16[4,768,768]{2,1,0:T(8,128)(2,1)S(1)}, bf16[4,768,768]{2,1,0:...) custom-call(s32[8]{0:T(128)S(1)} %copy-done.3, ...), custom_call_target="tpu_custom_call" | custom-call | flops 8000000000 | bytes 38000000 | tf_op jit(solution)/shard_map/build/pallas_call | solution.py:572
  30.8 0.0 collective-permute-done.3.x3_ref
  30.8 0.0 collective-permute-done.2.x2_ref
  30.8 0.0 collective-permute-done.1.x1_ref
  30.9 24.8 %chain.1.own = f32[4,144,768]{2,1,0:T(8,128)S(1)} custom-call(s32[8]{0:T(128)S(1)} %copy-done.4, bf16[128,768]{1,0:T(8,128)(2,1)S(1)} %copy-done.1, bf16[128,768]{1,0:T(8,128)(2,1)S(1)} %collective-permute-done.1.x1_ref, bf16[128,768]{1,0:T(8,128)(2,1)S(1)} %collective-permute-done.2.x2_ref, bf16[128,768]{1,0:T(8,128)(2,1)S(1)} %collective-permute-done.3.x3_ref, ...), custom_call_target="tpu_custom_call" | custom-call | flops 35000000512 | bytes 38000000 | tf_op jit(solution)/shard_map/chain/pallas_call | solution.py:596
  55.6 0.0 all-to-all-done.shared_ref
  55.7 1.5 %dots.1 = (f32[4,128,768]{2,1,0:T(8,128)S(1)}, f32[8,768]{1,0:T(8,128)S(1)}, f32[32,8,128]{2,1,0:T(8,128)S(1)}, f32[32,128]{1,0:T(8,128)S(1)}) custom-call(s32[8]{0:T(128)S(1)} %copy-done.4, f32[4,144,768]{2,1,0:T(8,128)S(1)} %chain.1.own, bf16[128,768]{1,0:T(8,128)(2,1)S(1)} %copy-done.1, f32[32,2,128]{2,1,0:T(2,128)S(1)} %all-to-all-done.shared_ref, ...), custom_call_target="tpu_custom_call" | custom-call | tf_op jit(solution)/shard_map/dots/pallas_call | solution.py:613
  57.2 13.4 %all_to_all.10.gram_ref = f32[32,8,128]{2,1,0:T(8,128)S(1)} all-to-all(f32[32,8,128]{2,1,0:T(8,128)S(1)} %get-tuple-element.43), channel_id=1, replica_groups=mesh['sub'=8,'grp'=4] {'sub','grp'}, dimensions={0} | all-to-all | bytes 262144 | tf_op jit(solution)/shard_map/all_to_all | solution.py:628
  70.6 2.2 %finish.1 = (f32[750,1,128]{2,1,0:T(1,128)}, f32[750,1,128]{2,1,0:T(1,128)}) custom-call(s32[8]{0:T(128)S(1)} %copy-done.4, f32[32,8,128]{2,1,0:T(8,128)S(1)} %all_to_all.10.gram_ref, f32[32,128]{1,0:T(8,128)S(1)} %get-tuple-element.44.inverse, f32[4,128,768]{2,1,0:T(8,128)S(1)} %get-tuple-element.45.fields_ref, f32[8,768]{1,0:T(8,128)S(1)} %get-tuple-element.46.images_ref, ...), custom_call_target="tpu_custom_call" | custom-call | tf_op jit(solution)/shard_map/finish/pallas_call | solution.py:629
  (10 shorter events, 0.0 us)
Async XLA Ops:
  2.7 17.7 %collective-permute-start.5 = (f32[8,768]{1,0:T(8,128)}, f32[8,768]{1,0:T(8,128)S(1)}, u32[]{:S(2)}, u32[]{:S(2)}) collective-permute-start(f32[8,768]{1,0:T(8,128)} %get-tuple-element.28.t0_ref), channel_id=1, source_target_pairs={{0,3},{1,2},{2,1},{3,0},{4,7},{5,6},{6,5},{7,4},{8,11},{9,10},{10,... | collective-permute-start | bytes 73736 | tf_op jit(solution)/shard_map/ppermute | solution.py:561
  7.8 13.6 %collective-permute-start.4 = (f32[8,768]{1,0:T(8,128)}, f32[8,768]{1,0:T(8,128)S(1)}, u32[]{:S(2)}, u32[]{:S(2)}) collective-permute-start(f32[8,768]{1,0:T(8,128)} %get-tuple-element.28.t0_ref), channel_id=1, source_target_pairs={{0,2},{1,3},{2,0},{3,1},{4,6},{5,7},{6,4},{7,5},{8,10},{9,11},{10,... | collective-permute-start | bytes 73736 | tf_op jit(solution)/shard_map/ppermute | solution.py:561
  7.8 10.8 %collective-permute-start = (f32[8,768]{1,0:T(8,128)}, f32[8,768]{1,0:T(8,128)S(1)}, u32[]{:S(2)}, u32[]{:S(2)}) collective-permute-start(f32[8,768]{1,0:T(8,128)} %get-tuple-element.28.t0_ref), channel_id=1, source_target_pairs={{0,1},{1,0},{2,3},{3,2},{4,5},{5,4},{6,7},{7,6},{8,9},{9,8},{10,11... | collective-permute-start | bytes 73736 | tf_op jit(solution)/shard_map/ppermute | solution.py:561
  8.4 22.3 %collective-permute-start.3 = (bf16[128,768]{1,0:T(8,128)(2,1)}, bf16[128,768]{1,0:T(8,128)(2,1)S(1)}, u32[]{:S(2)}, u32[]{:S(2)}) collective-permute-start(bf16[128,768]{1,0:T(8,128)(2,1)} %get-tuple-element.29.x0_ref), channel_id=1, source_target_pairs={{0,3},{1,2},{2,1},{3,0},{4,7},{5,6},{6,5},{7,4},{8,11},{9,10},{10,... | collective-permute-start | bytes 589832 | tf_op jit(solution)/shard_map/ppermute | solution.py:561
  12.2 18.6 %collective-permute-start.2 = (bf16[128,768]{1,0:T(8,128)(2,1)}, bf16[128,768]{1,0:T(8,128)(2,1)S(1)}, u32[]{:S(2)}, u32[]{:S(2)}) collective-permute-start(bf16[128,768]{1,0:T(8,128)(2,1)} %get-tuple-element.29.x0_ref), channel_id=1, source_target_pairs={{0,2},{1,3},{2,0},{3,1},{4,6},{5,7},{6,4},{7,5},{8,10},{9,11},{10,... | collective-permute-start | bytes 589832 | tf_op jit(solution)/shard_map/ppermute | solution.py:561
  12.2 43.5 %all-to-all-start = ((f32[32,2,128]{2,1,0:T(2,128)}), f32[32,2,128]{2,1,0:T(2,128)S(1)}, u32[]{:S(2)}, u32[]{:S(2)}) async-start(f32[32,2,128]{2,1,0:T(2,128)} %get-tuple-element.41), calls=%async_computation | async-start | bytes 65536 | tf_op jit(solution)/shard_map/all_to_all | solution.py:567
  18.6 12.2 %collective-permute-start.1 = (bf16[128,768]{1,0:T(8,128)(2,1)}, bf16[128,768]{1,0:T(8,128)(2,1)S(1)}, u32[]{:S(2)}, u32[]{:S(2)}) collective-permute-start(bf16[128,768]{1,0:T(8,128)(2,1)} %get-tuple-element.29.x0_ref), channel_id=1, source_target_pairs={{0,1},{1,0},{2,3},{3,2},{4,5},{5,4},{6,7},{7,6},{8,9},{9,8},{10,11... | collective-permute-start | bytes 589832 | tf_op jit(solution)/shard_map/ppermute | solution.py:561
  21.4 0.6 copy-start.3
  22.0 0.7 %copy-start.5 = (f32[8,768]{1,0:T(8,128)S(1)}, f32[8,768]{1,0:T(8,128)}, u32[]{:S(2)}) copy-start(f32[8,768]{1,0:T(8,128)} %get-tuple-element.28.t0_ref) | copy-start | bytes 73732
  22.8 8.1 %copy-start.1 = (bf16[128,768]{1,0:T(8,128)(2,1)S(1)}, bf16[128,768]{1,0:T(8,128)(2,1)}, u32[]{:S(2)}) copy-start(bf16[128,768]{1,0:T(8,128)(2,1)} %get-tuple-element.29.x0_ref) | copy-start | bytes 589828
  22.8 8.1 %copy-start.4 = (s32[8]{0:T(128)S(1)}, s32[8]{0:T(128)}, u32[]{:S(2)}) copy-start(s32[8]{0:T(128)} %get-tuple-element.26.order_ref) | copy-start | bytes 100
  30.8 24.8 %copy-start.2 = (f32[8,768]{1,0:T(8,128)S(1)}, f32[8,768]{1,0:T(8,128)}, u32[]{:S(2)}) copy-start(f32[8,768]{1,0:T(8,128)} %get-tuple-element.42.wide_ref) | copy-start | bytes 73732
  30.9 39.7 %copy-start = (f32[768,128]{1,0:T(8,128)S(1)}, f32[768,128]{1,0:T(8,128)}, u32[]{:S(2)}) copy-start(f32[768,128]{1,0:T(8,128)} %get-tuple-element.47.padded) | copy-start | bytes 1179652
